TPU v7x, 256 devices: a whole 4x4x8 slice. The times are simulated.
256 devices in a mesh: atom: 16 (over x, z_hi, core), refl: 16 (over z_lo, y).
Axes of the slice: x: 4, y: 4, z: 8 (z_hi: 2, z_lo: 4; z = z_hi * 4 + z_lo), core: 2. Of those that a mesh axis runs over, the one named last changes fastest.
Arguments:
- positions: float32 [3, 524288], P(None, ('atom', 'refl')), may hold values from 0 to 1
- occupancy: float32 [524288], P(('atom', 'refl')), may hold values from 0.3 to 1
- bfactor: float32 [524288], P(('atom', 'refl')), may hold values from 1 to 8
- atom_type: int32 [524288], P(('atom', 'refl')), may hold values from 0 to 7
- miller: int32 [3, 2048], P(None, 'refl'), may hold values from -48 to 48
- observed: float32 [2048], P('refl'), may hold values from 0.2 to 5
- weight: float32 [2048], P('refl'), may hold values from 0.3 to 3
- coef_a: float32 [8, 4], replicated, may hold values from 0.3 to 3
- coef_b: float32 [8, 4], replicated, may hold values from 0.5 to 20
- coef_c: float32 [8], replicated, may hold values from 0.1 to 1
Outputs:
- gradient: float32 [3, 524288], P(None, ('atom', 'refl'))
- residual: float32 [2048], P('refl')
All inputs are finite; a program needn't handle non-finite values.
Results may differ from a plain program's by a relative error of at most 0.0003.
Values sent between devices are 32-bit elements; how exact they have to be, the bound alone decides.
A program may use at most 64 MiB of HBM per device.

v0:
```python
import math

import jax
import jax.numpy as jnp
from jax import lax
from jax.sharding import PartitionSpec as P

two_pi = 6.283185307179586
cell_edge = 100.0


def form_table(coef_a, coef_b, coef_c, s2):
    return (
        jnp.sum(
            coef_a[:, :, None] * jnp.exp(-0.25 * coef_b[:, :, None] * s2[None, None, :]), axis=1
        )
        + coef_c[:, None]
    )


def block_terms(stack, hklf, s2, table):
    turns = (
        stack[0][:, None] * hklf[0][None]
        + stack[1][:, None] * hklf[1][None]
        + stack[2][:, None] * hklf[2][None]
    )
    phase = two_pi * turns
    kinds = (stack[5][:, None] == jnp.arange(table.shape[0], dtype=stack.dtype)[None]).astype(
        stack.dtype
    )
    form = jnp.dot(kinds, table, precision=lax.Precision.HIGHEST)
    weighted = stack[3][:, None] * jnp.exp(-0.25 * stack[4][:, None] * s2[None]) * form
    return (weighted, jnp.cos(phase), jnp.sin(phase))


def atom_blocks(stack):
    count = stack.shape[1]
    width = math.gcd(count, 512)
    return stack.reshape(stack.shape[0], count // width, width).transpose(1, 0, 2)


def forward_sum(stack, hklf, s2, table):

    def step(total, block):
        weighted, cosv, sinv = block_terms(block, hklf, s2, table)
        return (
            total + jnp.stack([jnp.sum(weighted * cosv, axis=0), jnp.sum(weighted * sinv, axis=0)]),
            None,
        )

    total, unused = lax.scan(step, jnp.zeros((2, hklf.shape[1]), jnp.float32), atom_blocks(stack))
    return total


def backward_terms(stack, hklf, s2, table, along_b, along_a):

    def one_block(block):
        weighted, cosv, sinv = block_terms(block, hklf, s2, table)
        inner = weighted * (along_b[None] * cosv - along_a[None] * sinv)
        return jnp.einsum("dr,nr->dn", hklf, inner, precision=lax.Precision.HIGHEST)

    terms = lax.map(one_block, atom_blocks(stack))
    return terms.transpose(1, 0, 2).reshape(3, stack.shape[1])


def amplitudes(sums, inv_atoms):
    real_part = sums[0] * inv_atoms
    imag_part = sums[1] * inv_atoms
    amp = jnp.sqrt(real_part * real_part + imag_part * imag_part + 0.25)
    return (real_part, imag_part, amp)


def local(
    positions, occupancy, bfactor, atom_type, miller, observed, weight, coef_a, coef_b, coef_c
):
    n_atom = lax.axis_size("atom")
    n_refl = lax.axis_size("refl")
    shard = positions.shape[1]
    rows_dev = miller.shape[1]
    total_atoms = shard * n_atom * n_refl
    total_refl = rows_dev * n_refl
    inv_atoms = 1.0 / math.sqrt(total_atoms)
    root_refl = math.sqrt(total_refl)
    stack = jnp.concatenate(
        [positions, occupancy[None], bfactor[None], atom_type.astype(jnp.float32)[None]], axis=0
    )
    hklf = miller.astype(jnp.float32)
    rows = jnp.concatenate([hklf, observed[None], weight[None]], axis=0)
    every = lax.all_gather(rows, "refl", axis=1, tiled=True)
    all_hkl = every[0:3]
    all_obs = every[3]
    all_weight = every[4]
    s2 = jnp.sum(all_hkl * all_hkl, axis=0) / (cell_edge * cell_edge)
    table = form_table(coef_a, coef_b, coef_c, s2)
    partial_sums = forward_sum(stack, all_hkl, s2, table)
    sums = lax.psum(partial_sums, ("atom", "refl"))
    real_part, imag_part, amp = amplitudes(sums, inv_atoms)
    scale = jnp.sum(all_weight * all_obs * amp) / jnp.sum(all_weight * amp * amp)
    resid_all = scale * amp - all_obs
    coeff = 2.0 * all_weight * scale * resid_all / (amp * root_refl)
    along_b = coeff * imag_part
    along_a = coeff * real_part
    terms = backward_terms(stack, all_hkl, s2, table, along_b, along_a)
    gradient = terms * (two_pi * inv_atoms)
    offset = lax.axis_index("refl") * rows_dev
    residual = lax.dynamic_slice_in_dim(resid_all, offset, rows_dev, 0)
    return (gradient, residual)


def solution(mesh):
    placed = (
        P(None, ("atom", "refl")),
        P(("atom", "refl")),
        P(("atom", "refl")),
        P(("atom", "refl")),
        P(None, "refl"),
        P("refl"),
        P("refl"),
        P(),
        P(),
        P(),
    )
    return jax.shard_map(
        local,
        mesh=mesh,
        in_specs=placed,
        out_specs=(P(None, ("atom", "refl")), P("refl")),
        check_vma=False,
    )
```

profile of v0, /device:TPU:1, one launch (start us, length us, event | category | flops | bytes accessed | tf_op | source)
XLA Modules:
  0.0 293.8 jit_solution(7289391292286830051)
XLA Ops:
  0.6 0.7 convert_element_type.9
  1.3 0.7 pad_maximum_fusion
  2.0 0.7 broadcast_multiply_fusion.2
  2.7 0.7 convert_element_type.8
  3.4 0.8 maximum_bitcast_fusion
  4.2 37.7 %all_gather.3 = f32[5,2048]{1,0:T(8,128)S(1)} all-gather(f32[5,128]{1,0:T(8,128)S(1)} %pad_maximum_fusion), channel_id=1, replica_groups=mesh['atom'=16,'refl'=16] {'refl'}, dimensions={1}, use_global_device_ids=true | all-gather | bytes 43520 | tf_op jit(solution)/shard_map/all_gather | solution.py:89
  42.0 0.8 multiply_reduce_fusion.2
  42.8 0.7 broadcast_add_fusion
  43.5 76.9 %while.22 = (s32[]{:T(128)}, f32[2,2048]{1,0:T(2,128)S(1)}, f32[4,6,512]{2,1,0:T(8,128)S(1)}, f32[2048]{0:T(1024)S(1)}, f32[8,2048]{1,0:T(8,128)S(1)}, /*index=5...) while((s32[]{:T(128)}, f32[2,2048]{1,0:T(2,128)S(1)}, ...), condition=%wide.region_5.6_spmd.clone, body=%wide.region_2.5_spmd.clone.sunk | while | flops 114307592 | bytes 250083 | solution.py:51
  43.6 19.1 %multiply_reduce_fusion.6 = (f32[2048]{0:T(1024)S(1)}, f32[2048]{0:T(1024)S(1)}) fusion(f32[2048]{0:T(1024)S(1)} %bitcast.99, f32[512]{0:T(512)S(1)} %bitcast.114, f32[2048]{0:T(1024)S(1)} %bitcast.100, f32[512]{0:T(512)S(1)} %bitcast.110, f32[2048]{0:T(1024)S(1)} %bitcast.98, f32[512]{0:T(512)S(1)} %bitcast.109, ...), kind=kOutput, calls=%fused_computation.42.clone.1 | convolution fusion | flops 114294784 | bytes 126976 | tf_op jit(solution)/shard_map/while/body/eval_jaxpr/dot_general | solution.py:31
  62.8 19.1 %multiply_reduce_fusion.6 = (f32[2048]{0:T(1024)S(1)}, f32[2048]{0:T(1024)S(1)}) fusion(f32[2048]{0:T(1024)S(1)} %bitcast.99, f32[512]{0:T(512)S(1)} %bitcast.114, f32[2048]{0:T(1024)S(1)} %bitcast.100, f32[512]{0:T(512)S(1)} %bitcast.110, f32[2048]{0:T(1024)S(1)} %bitcast.98, f32[512]{0:T(512)S(1)} %bitcast.109, ...), kind=kOutput, calls=%fused_computation.42.clone.1 | convolution fusion | flops 114294784 | bytes 126976 | tf_op jit(solution)/shard_map/while/body/eval_jaxpr/dot_general | solution.py:31
  82.0 19.1 %multiply_reduce_fusion.6 = (f32[2048]{0:T(1024)S(1)}, f32[2048]{0:T(1024)S(1)}) fusion(f32[2048]{0:T(1024)S(1)} %bitcast.99, f32[512]{0:T(512)S(1)} %bitcast.114, f32[2048]{0:T(1024)S(1)} %bitcast.100, f32[512]{0:T(512)S(1)} %bitcast.110, f32[2048]{0:T(1024)S(1)} %bitcast.98, f32[512]{0:T(512)S(1)} %bitcast.109, ...), kind=kOutput, calls=%fused_computation.42.clone.1 | convolution fusion | flops 114294784 | bytes 126976 | tf_op jit(solution)/shard_map/while/body/eval_jaxpr/dot_general | solution.py:31
  101.3 19.1 %multiply_reduce_fusion.6 = (f32[2048]{0:T(1024)S(1)}, f32[2048]{0:T(1024)S(1)}) fusion(f32[2048]{0:T(1024)S(1)} %bitcast.99, f32[512]{0:T(512)S(1)} %bitcast.114, f32[2048]{0:T(1024)S(1)} %bitcast.100, f32[512]{0:T(512)S(1)} %bitcast.110, f32[2048]{0:T(1024)S(1)} %bitcast.98, f32[512]{0:T(512)S(1)} %bitcast.109, ...), kind=kOutput, calls=%fused_computation.42.clone.1 | convolution fusion | flops 114294784 | bytes 126976 | tf_op jit(solution)/shard_map/while/body/eval_jaxpr/dot_general | solution.py:31
  120.4 81.0 %psum.7 = f32[2,2048]{1,0:T(2,128)S(1)} all-reduce(f32[2,2048]{1,0:T(2,128)S(1)} %get-tuple-element.76), channel_id=1, replica_groups=mesh['atom'=16,'refl'=16] {'atom','refl'}, use_global_device_ids=true, to_apply=%region_6.7 | all-reduce | flops 4096 | bytes 32768 | tf_op jit(solution)/shard_map/psum | solution.py:96
  201.5 0.7 fusion.39
  203.6 0.6 dynamic_slice.10
  204.2 89.0 %while.21 = (s32[]{:T(128)}, f32[4,3,512]{2,1,0:T(4,128)S(1)}, f32[4,6,512]{2,1,0:T(8,128)S(1)}, f32[2048]{0:T(1024)S(1)}, f32[8,2048]{1,0:T(8,128)S(1)}, /*inde...) while((s32[]{:T(128)}, f32[4,3,512]{2,1,0:T(4,128)S(1)}, ...), condition=%wide.region_10.11_spmd, body=%wide.region_9.10_spmd.sunk | while | flops 152048128 | bytes 8630509 | solution.py:62
  204.2 1.8 fusion.59
  206.1 20.3 %fusion.61 = f32[4,3,512]{2,1,0:T(4,128)S(1)} fusion(f32[4,3,512]{2,1,0:T(4,128)S(1)} %get-tuple-element.340, s32[]{:T(128)S(6)} %copy.25, f32[3,2048]{1,0:T(4,128)S(1)} %get-tuple-element.360, f32[512,2048]{1,0:T(8,128)S(1)} %fusion.59, f32[2048]{0:T(1024)S(1)} %get-tuple-element.361, f32[2048]{0:T(1024)S(1)} %bitcast.96, f32[512]{0:T(512)S(1)} %bitcast.119, ...), kind=kOutput, calls=%fused_computation.30.clone.1 | convolution fusion | flops 51380224 | bytes 4294660 | tf_op jit(solution)/shard_map/while/body/eval_jaxpr/dr,nr->dn/dot_general | solution.py:60
  226.5 1.8 fusion.59
  228.3 20.3 %fusion.61 = f32[4,3,512]{2,1,0:T(4,128)S(1)} fusion(f32[4,3,512]{2,1,0:T(4,128)S(1)} %get-tuple-element.340, s32[]{:T(128)S(6)} %copy.25, f32[3,2048]{1,0:T(4,128)S(1)} %get-tuple-element.360, f32[512,2048]{1,0:T(8,128)S(1)} %fusion.59, f32[2048]{0:T(1024)S(1)} %get-tuple-element.361, f32[2048]{0:T(1024)S(1)} %bitcast.96, f32[512]{0:T(512)S(1)} %bitcast.119, ...), kind=kOutput, calls=%fused_computation.30.clone.1 | convolution fusion | flops 51380224 | bytes 4294660 | tf_op jit(solution)/shard_map/while/body/eval_jaxpr/dr,nr->dn/dot_general | solution.py:60
  248.7 1.8 fusion.59
  250.6 20.3 %fusion.61 = f32[4,3,512]{2,1,0:T(4,128)S(1)} fusion(f32[4,3,512]{2,1,0:T(4,128)S(1)} %get-tuple-element.340, s32[]{:T(128)S(6)} %copy.25, f32[3,2048]{1,0:T(4,128)S(1)} %get-tuple-element.360, f32[512,2048]{1,0:T(8,128)S(1)} %fusion.59, f32[2048]{0:T(1024)S(1)} %get-tuple-element.361, f32[2048]{0:T(1024)S(1)} %bitcast.96, f32[512]{0:T(512)S(1)} %bitcast.119, ...), kind=kOutput, calls=%fused_computation.30.clone.1 | convolution fusion | flops 51380224 | bytes 4294660 | tf_op jit(solution)/shard_map/while/body/eval_jaxpr/dr,nr->dn/dot_general | solution.py:60
  271.0 1.8 fusion.59
  272.8 20.3 %fusion.61 = f32[4,3,512]{2,1,0:T(4,128)S(1)} fusion(f32[4,3,512]{2,1,0:T(4,128)S(1)} %get-tuple-element.340, s32[]{:T(128)S(6)} %copy.25, f32[3,2048]{1,0:T(4,128)S(1)} %get-tuple-element.360, f32[512,2048]{1,0:T(8,128)S(1)} %fusion.59, f32[2048]{0:T(1024)S(1)} %get-tuple-element.361, f32[2048]{0:T(1024)S(1)} %bitcast.96, f32[512]{0:T(512)S(1)} %bitcast.119, ...), kind=kOutput, calls=%fused_computation.30.clone.1 | convolution fusion | flops 51380224 | bytes 4294660 | tf_op jit(solution)/shard_map/while/body/eval_jaxpr/dr,nr->dn/dot_general | solution.py:60
  293.1 0.6 broadcast_multiply_fusion
  (28 shorter events, 0.6 us)
where the time goes:
time: 294 us
  matrix products  165 us (56%)
  blocking collectives  119 us (40%)
  other arithmetic  6.87 us (2%)
    dot_general x8, matrix products, block_terms(): form = jnp.dot(kinds, table, precision=lax.Precision.HIGHEST)  83.8 us
    dot_general x4, matrix products, one_block(): return jnp.einsum('dr,nr->dn', hklf, inner, precision=lax.Precision.HIGHEST)  81.3 us
    psum x1, blocking collectives, local(): sums = lax.psum(partial_sums, ('atom', 'refl'))  81 us
    all_gather x1, blocking collectives, local(): every = lax.all_gather(rows, 'refl', axis=1, tiled=True)  37.7 us

commit v1 on v0

v1 whole, which is shorter than its diff:
```python
import functools
import math

import jax
import jax.numpy as jnp
from jax import lax
from jax.experimental import pallas as pl
from jax.experimental.pallas import tpu as pltpu
from jax.sharding import PartitionSpec as P

MESH = pl.DeviceIdType.MESH
two_pi = 6.283185307179586
cell_edge = 100.0
top = 48
TYPES, GAUSS = 8, 4
LANES = 128
unroll_f, unroll_b = 32, 32


def rotate(ac, as_, bc, bs):
    return ac * bc - as_ * bs, ac * bs + as_ * bc


def fold_rows(vregs):
    row = lax.broadcasted_iota(jnp.int32, (8, LANES), 0)
    for shift in (4, 2, 1):
        low = (row & shift) == 0
        half = len(vregs) // 2
        merged = []
        for n in range(half):
            a, b = vregs[n], vregs[n + half]
            keep = jnp.where(low, a, b)
            if shift == 4:
                move = pltpu.roll(jnp.where(low, b, a), 4, 0)
            else:
                move = jnp.where(low, pltpu.roll(a, 8 - shift, 0), pltpu.roll(b, shift, 0))
            merged.append(keep + move)
        vregs = merged
    return vregs[0]


def kernel(
    n_atom, n_refl,
    pos_ref, occ_ref, bf_ref, type_ref, miller_ref, obs_ref, weight_ref, ca_ref, cb_ref, cc_ref,
    grad_ref, resid_ref,
    tx, ty, tz, store, form_rows, form_t, rows, idx_v, hs, ks, ls, sums, part, reduced, mine, total_in, every,
    bu, bv, bh, bk, bl,
    g_send, g_recv, r_send, r_recv, a_send, a_recv, e_send, e_recv, i_sem,
):
    me_a = lax.axis_index("atom")
    me_r = lax.axis_index("refl")
    tiles = occ_ref.shape[0]
    refl = n_refl * LANES

    barrier = pltpu.get_barrier_semaphore()

    def greet(s, _):
        pl.semaphore_signal(barrier, inc=1, device_id=(me_a, lax.rem(me_r + s, n_refl)), device_id_type=MESH)
        return 0

    def greet_a(s, _):
        pl.semaphore_signal(barrier, inc=1, device_id=(lax.rem(me_a + s, n_atom), me_r), device_id_type=MESH)
        return 0

    lax.fori_loop(1, n_refl, greet, 0)
    lax.fori_loop(1, n_atom, greet_a, 0)

    rows[me_r] = miller_ref[...]

    pl.semaphore_wait(barrier, n_refl - 1 + n_atom - 1)

    def gather_copy(s):
        peer = lax.rem(me_r + s, n_refl)
        return pltpu.make_async_remote_copy(
            src_ref=rows.at[me_r], dst_ref=rows.at[me_r],
            send_sem=g_send.at[peer], recv_sem=g_recv.at[me_r],
            device_id=(me_a, peer), device_id_type=MESH,
        )

    def gather_wait(s):
        peer = lax.rem(me_r + s, n_refl)
        return pltpu.make_async_remote_copy(
            src_ref=rows.at[me_r], dst_ref=rows.at[peer],
            send_sem=g_send.at[peer], recv_sem=g_recv.at[peer],
            device_id=(me_a, peer), device_id_type=MESH,
        )

    def g_start(s, _):
        gather_copy(s).start()
        return 0

    lax.fori_loop(1, n_refl, g_start, 0)

    first = []
    for d in range(3):
        x = jnp.concatenate([pos_ref[d : d + 1, a * LANES : (a + 1) * LANES] for a in range(tiles)], axis=0)
        turn = two_pi * (x - jnp.round(x))
        first.append((jnp.cos(turn), jnp.sin(turn)))
    decay = bf_ref[...] * (-0.25 / (cell_edge * cell_edge))
    occ = occ_ref[...]

    def table_step(m, carry):
        mf = m.astype(jnp.float32)
        damp = jnp.exp(decay * (mf * mf))
        after = []
        for d, table in enumerate((tx, ty, tz)):
            c, s = carry[2 * d], carry[2 * d + 1]
            scale = damp * occ if d == 2 else damp
            table[top + m, 0] = c * scale
            table[top + m, 1] = s * scale
            table[top - m, 0] = c * scale
            table[top - m, 1] = -(s * scale)
            after += list(rotate(c, s, *first[d]))
        return tuple(after)

    one = jnp.ones((tiles, LANES), jnp.float32)
    zero = jnp.zeros((tiles, LANES), jnp.float32)
    lax.fori_loop(0, top + 1, table_step, (one, zero) * 3)

    def g_wait(s, _):
        gather_wait(s).wait_recv()
        return 0

    lax.fori_loop(1, n_refl, g_wait, 0)

    for d in range(3):
        for b in range(n_refl):
            idx_v[d, :, b * LANES : (b + 1) * LANES] = rows[b, d : d + 1, :] + top
    to_smem = [
        pltpu.make_async_copy(idx_v.at[d, 0], dst, i_sem.at[d]) for d, dst in enumerate((hs, ks, ls))
    ]
    for copy in to_smem:
        copy.start()

    hf, kf, lf = (rows[:, d, :].astype(jnp.float32) for d in range(3))
    s2 = (hf * hf + kf * kf + lf * lf) / (cell_edge * cell_edge)
    for t in range(TYPES):
        form = ca_ref[t, 0] * jnp.exp(-0.25 * cb_ref[t, 0] * s2)
        for g in range(1, GAUSS):
            form = form + ca_ref[t, g] * jnp.exp(-0.25 * cb_ref[t, g] * s2)
        form_t[:, t, :] = form + cc_ref[t]
    pad = jnp.zeros((LANES - TYPES, LANES), jnp.float32)
    for b in range(n_refl):
        form_rows[b * LANES : (b + 1) * LANES, :] = jnp.concatenate([form_t[b], pad], axis=0).T

    for copy in to_smem:
        copy.wait()

    kind = [type_ref[v * 8 : (v + 1) * 8, :] for v in range(tiles // 8)]

    def reduce_copy(b):
        return pltpu.make_async_remote_copy(
            src_ref=part.at[b], dst_ref=reduced.at[me_r],
            send_sem=r_send.at[b], recv_sem=r_recv.at[me_r],
            device_id=(me_a, b), device_id_type=MESH,
        )

    def reduce_wait(b):
        return pltpu.make_async_remote_copy(
            src_ref=part.at[b], dst_ref=reduced.at[b],
            send_sem=r_send.at[b], recv_sem=r_recv.at[b],
            device_id=(me_a, b), device_id_type=MESH,
        )

    def forward_block(step, _):
        b = lax.rem(me_r + 1 + step, n_refl)
        base = pl.multiple_of(b * LANES, LANES)

        def chunk(i, _):
            local0 = pl.multiple_of(i * unroll_f, unroll_f)
            r0 = base + local0
            parts = []
            for u in range(unroll_f):
                r = r0 + u
                h, k, l = hs[r], ks[r], ls[r]
                form_row = jnp.broadcast_to(form_rows[pl.ds(r, 1), :], (8, LANES))
                real, imag = None, None
                for v in range(tiles // 8):
                    off = v * 8
                    c, s = rotate(
                        tx[h, 0, off : off + 8, :], tx[h, 1, off : off + 8, :],
                        ty[k, 0, off : off + 8, :], ty[k, 1, off : off + 8, :],
                    )
                    c, s = rotate(c, s, tz[l, 0, off : off + 8, :], tz[l, 1, off : off + 8, :])
                    form = jnp.take_along_axis(form_row, kind[v], axis=1, mode="promise_in_bounds")
                    c = c * form
                    s = s * form
                    store[r, 0, off : off + 8, :] = c
                    store[r, 1, off : off + 8, :] = s
                    real = c if real is None else real + c
                    imag = s if imag is None else imag + s
                parts.append((real, imag))
            for g in range(unroll_f // 8):
                for j in range(2):
                    sums[j, pl.ds(local0 + g * 8, 8), :] = fold_rows([parts[g * 8 + u][j] for u in range(8)])
            return 0

        lax.fori_loop(0, LANES // unroll_f, chunk, 0)
        for j in range(2):
            part[b, j : j + 1, :] = jnp.sum(sums[j].T, axis=0, keepdims=True)

        @pl.when(step < n_refl - 1)
        def _():
            reduce_copy(b).start()

        return 0

    lax.fori_loop(0, n_refl, forward_block, 0)
    reduced[me_r] = part[me_r]

    def r_wait(s, _):
        reduce_wait(lax.rem(me_r + s, n_refl)).wait_recv()
        return 0

    lax.fori_loop(1, n_refl, r_wait, 0)
    mine[...] = jnp.sum(reduced[...], axis=0)
    total_in[me_a] = mine[...]

    def atom_copy(s, slot):
        peer = lax.rem(me_a + s, n_atom)
        return pltpu.make_async_remote_copy(
            src_ref=mine, dst_ref=total_in.at[me_a if slot is None else peer],
            send_sem=a_send.at[peer], recv_sem=a_recv.at[me_a if slot is None else peer],
            device_id=(peer, me_r), device_id_type=MESH,
        )

    def a_start(s, _):
        atom_copy(s, None).start()
        return 0

    def a_wait(s, _):
        atom_copy(s, 1).wait_recv()
        return 0

    lax.fori_loop(1, n_atom, a_start, 0)

    for b in range(n_refl):
        for d, wide in enumerate((bh, bk, bl)):
            wide[b * LANES : (b + 1) * LANES, :] = jnp.broadcast_to(rows[b, d : d + 1, :].astype(jnp.float32), (LANES, LANES)).T

    lax.fori_loop(1, n_atom, a_wait, 0)
    every[me_r, 0:2, :] = jnp.sum(total_in[...], axis=0)
    every[me_r, 2:3, :] = obs_ref[...]
    every[me_r, 3:4, :] = weight_ref[...]

    def every_copy(s, slot):
        peer = lax.rem(me_r + s, n_refl)
        return pltpu.make_async_remote_copy(
            src_ref=every.at[me_r], dst_ref=every.at[me_r if slot is None else peer],
            send_sem=e_send.at[peer], recv_sem=e_recv.at[me_r if slot is None else peer],
            device_id=(me_a, peer), device_id_type=MESH,
        )

    def e_start(s, _):
        every_copy(s, None).start()
        return 0

    def e_wait(s, _):
        every_copy(s, 1).wait_recv()
        return 0

    lax.fori_loop(1, n_refl, e_start, 0)
    lax.fori_loop(1, n_refl, e_wait, 0)

    atoms = tiles * LANES * n_atom * n_refl
    inv_atoms = 1.0 / math.sqrt(atoms)
    real_part = every[:, 0, :] * inv_atoms
    imag_part = every[:, 1, :] * inv_atoms
    amp = jnp.sqrt(real_part * real_part + imag_part * imag_part + 0.25)
    obs = every[:, 2, :]
    weight = every[:, 3, :]
    over = jnp.sum(weight * obs * amp, axis=(0, 1), keepdims=True)
    under = jnp.sum(weight * amp * amp, axis=(0, 1), keepdims=True)
    scale = over / under
    resid = scale * amp - obs
    coeff = 2.0 * weight * scale * resid / (amp * math.sqrt(refl)) * (two_pi * inv_atoms)
    along_b = coeff * imag_part
    along_a = coeff * real_part
    sums[0, 0:n_refl, :] = resid
    resid_ref[...] = sums[0, pl.ds(me_r, 1), :]
    for b in range(n_refl):
        bu[b * LANES : (b + 1) * LANES, :] = jnp.broadcast_to(along_b[b : b + 1, :], (LANES, LANES)).T
        bv[b * LANES : (b + 1) * LANES, :] = jnp.broadcast_to(along_a[b : b + 1, :], (LANES, LANES)).T

    def backward_chunk(i, acc):
        acc = [list(a) for a in acc]
        r0 = pl.multiple_of(i * unroll_b, unroll_b)
        for u in range(unroll_b):
            r = r0 + u
            wide = [jnp.broadcast_to(w[pl.ds(r, 1), :], (8, LANES)) for w in (bu, bv, bh, bk, bl)]
            for v in range(tiles // 8):
                off = v * 8
                inner = wide[0] * store[r, 0, off : off + 8, :] - wide[1] * store[r, 1, off : off + 8, :]
                for d in range(3):
                    acc[d][v] = acc[d][v] + wide[2 + d] * inner
        return tuple(tuple(a) for a in acc)

    none = jnp.zeros((8, LANES), jnp.float32)
    acc = lax.fori_loop(0, refl // unroll_b, backward_chunk, ((none,) * (tiles // 8),) * 3)
    for d in range(3):
        for v in range(tiles // 8):
            for a in range(8):
                t = v * 8 + a
                grad_ref[d : d + 1, t * LANES : (t + 1) * LANES] = acc[d][v][a : a + 1, :]

    def finish(s, _):
        gather_wait(s).wait_send()
        reduce_wait(lax.rem(me_r + s, n_refl)).wait_send()
        every_copy(s, 1).wait_send()
        return 0

    def finish_a(s, _):
        atom_copy(s, 1).wait_send()
        return 0

    lax.fori_loop(1, n_refl, finish, 0)
    lax.fori_loop(1, n_atom, finish_a, 0)


def solution(mesh):
    n_atom, n_refl = mesh.shape["atom"], mesh.shape["refl"]

    def local(positions, occupancy, bfactor, atom_type, miller, observed, weight, coef_a, coef_b, coef_c):
        shard = positions.shape[1]
        tiles = shard // LANES
        refl = miller.shape[1] * n_refl
        vmem = pl.BlockSpec(memory_space=pltpu.VMEM)
        smem = pl.BlockSpec(memory_space=pltpu.SMEM)
        f32 = jnp.float32
        table = pltpu.VMEM((2 * top + 1, 2, tiles, LANES), f32)
        wide = pltpu.VMEM((refl, LANES), f32)
        pair_r = pltpu.VMEM((n_refl, 2, LANES), f32)
        dma_r = pltpu.SemaphoreType.DMA((n_refl,))
        dma_a = pltpu.SemaphoreType.DMA((n_atom,))
        gradient, residual = pl.pallas_call(
            functools.partial(kernel, n_atom, n_refl),
            out_shape=(
                jax.ShapeDtypeStruct((3, shard), f32),
                jax.ShapeDtypeStruct((1, LANES), f32),
            ),
            in_specs=[vmem] * 7 + [smem] * 3,
            out_specs=(vmem, vmem),
            scratch_shapes=[
                table, table, table,
                pltpu.VMEM((refl, 2, tiles, LANES), f32),
                wide,
                pltpu.VMEM((n_refl, TYPES, LANES), f32),
                pltpu.VMEM((n_refl, 3, LANES), jnp.int32),
                pltpu.VMEM((3, 1, refl), jnp.int32),
                pltpu.SMEM((refl,), jnp.int32),
                pltpu.SMEM((refl,), jnp.int32),
                pltpu.SMEM((refl,), jnp.int32),
                pltpu.VMEM((2, LANES, LANES), f32),
                pair_r, pair_r,
                pltpu.VMEM((2, LANES), f32),
                pltpu.VMEM((n_atom, 2, LANES), f32),
                pltpu.VMEM((n_refl, 4, LANES), f32),
                wide, wide, wide, wide, wide,
                dma_r, dma_r, dma_r, dma_r, dma_a, dma_a, dma_r, dma_r,
                pltpu.SemaphoreType.DMA((3,)),
            ],
            compiler_params=pltpu.CompilerParams(
                collective_id=0, has_side_effects=True, vmem_limit_bytes=58 * 2**20
            ),
        )(
            positions,
            occupancy.reshape(tiles, LANES),
            bfactor.reshape(tiles, LANES),
            atom_type.reshape(tiles, LANES),
            miller,
            observed.reshape(1, LANES),
            weight.reshape(1, LANES),
            coef_a, coef_b, coef_c,
        )
        return gradient, residual.reshape(LANES)

    split = P(("atom", "refl"))
    return jax.shard_map(
        local,
        mesh=mesh,
        in_specs=(
            P(None, ("atom", "refl")), split, split, split,
            P(None, "refl"), P("refl"), P("refl"), P(), P(), P(),
        ),
        out_specs=(P(None, ("atom", "refl")), P("refl")),
        check_vma=False,
    )
```

time: 294 us -> 59.2 us (0.20)
  matrix products: 165 us -> 0 us
  blocking collectives: 119 us -> 0 us
  Pallas kernels: 0 us -> 54.3 us
  other arithmetic: 6.87 us -> 0 us
  local copies, waits for them, and re-layouts: 0.76 us -> 3.92 us
    dot_general x12 -> x0, matrix products: 165 us -> none  [the longest x8 83.8 us: block_terms(): form = jnp.dot(kinds, table, precision=lax.Precision.HIGHEST)]
    psum x1 -> x0, blocking collectives: 81 us -> none  [local(): sums = lax.psum(partial_sums, ('atom', 'refl'))]
    pallas_call x0 -> x1, Pallas kernels: none -> 54.3 us  [local(): pl.pallas_call(functools.partial(kernel, n_atom, n_refl), out_shape=(jax....]
    all_gather x1 -> x0, blocking collectives: 37.7 us -> none  [local(): every = lax.all_gather(rows, 'refl', axis=1, tiled=True)]
    unnamed x0 -> x10, local copies, waits for them, and re-layouts: none -> 3.92 us
where the time goes in v1:
time: 59.2 us; the launch traced here: 58.9 us
  Pallas kernels  54.3 us (92%)
  local copies, waits for them, and re-layouts  3.92 us (7%)
  between operations  0.66 us (1%)
    pallas_call x1, Pallas kernels, local(): pl.pallas_call(functools.partial(kernel, n_atom, n_refl), out_shape=(jax....  54.3 us
    unnamed x10, local copies, waits for them, and re-layouts  3.92 us

profile of v1, /device:TPU:1, one launch (start us, length us, event | category | flops | bytes accessed | tf_op | source)
XLA Modules:
  0.0 58.9 jit_solution(17473595348493512986)
XLA Ops:
  0.6 0.0 copy-start
  0.6 0.7 %copy-done = f32[8,4]{0,1:T(4,128)S(1)} copy-done((f32[8,4]{0,1:T(4,128)S(1)}, f32[8,4]{0,1:T(4,128)}, u32[]{:S(2)}) %copy-start) | copy-done | bytes 152
  1.3 0.0 copy-start.1
  1.3 0.7 %copy.12.ca_ref = f32[8,4]{1,0:T(8,128)} copy(f32[8,4]{0,1:T(4,128)S(1)} %copy-done) | data formatting | bytes 256 | tf_op args[7]
  2.0 0.0 copy-done.1
  2.0 0.7 %copy.13.cb_ref = f32[8,4]{1,0:T(8,128)} copy(f32[8,4]{0,1:T(4,128)S(1)} %copy-done.1) | data formatting | bytes 256 | tf_op args[8]
  2.7 54.3 %shard_map.113 = (f32[3,2048]{1,0:T(4,128)}, f32[1,128]{1,0:T(1,128)}) custom-call(f32[3,2048]{1,0:T(4,128)} %pos_ref.1, f32[16,128]{1,0:T(8,128)} %bitcast.6, f32[16,128]{1,0:T(8,128)} %bitcast.7, s32[16,128]{1,0:T(8,128)} %bitcast.8, s32[3,128]{1,0:T(4,128)} %miller_ref.1, f32[1,128]{1,0:T(1,128)} %bitcast.9, f32[1,128]{1,0:T(1,128)} %bitcast.10, ...), custom_call_target="tpu_custom_call" | custom-call | tf_op jit(solution)/shard_map/pallas_call | solution.py:335
  57.0 0.0 copy-start.2
  57.0 1.4 %copy.16 = f32[3,2048]{1,0:T(4,128)} copy(f32[3,2048]{1,0:T(4,128)} %get-tuple-element.8) | data formatting | bytes 49152
  58.4 0.0 copy-done.2
  58.4 0.5 copy.17
Async XLA Ops:
  0.6 0.7 %copy-start = (f32[8,4]{0,1:T(4,128)S(1)}, f32[8,4]{0,1:T(4,128)}, u32[]{:S(2)}) copy-start(f32[8,4]{0,1:T(4,128)} %param.17) | copy-start | bytes 388
  1.3 0.7 %copy-start.1 = (f32[8,4]{0,1:T(4,128)S(1)}, f32[8,4]{0,1:T(4,128)}, u32[]{:S(2)}) copy-start(f32[8,4]{0,1:T(4,128)} %param.18) | copy-start | bytes 388
  57.0 1.4 %copy-start.2 = (f32[1,128]{1,0:T(1,128)S(1)}, f32[1,128]{1,0:T(1,128)}, u32[]{:S(2)}) copy-start(f32[1,128]{1,0:T(1,128)} %get-tuple-element.5) | copy-start | bytes 1540

commit v2 on v1

v2 whole, which is shorter than its diff:
```python
import functools
import math

import jax
import jax.numpy as jnp
from jax import lax
from jax.experimental import pallas as pl
from jax.experimental.pallas import tpu as pltpu
from jax.sharding import PartitionSpec as P

MESH = pl.DeviceIdType.MESH
two_pi = 6.283185307179586
cell_edge = 100.0
top = 48
TYPES, GAUSS = 8, 4
LANES = 128
unroll_b = 32


def rotate(ac, as_, bc, bs):
    return ac * bc - as_ * bs, ac * bs + as_ * bc


def kernel(
    n_atom, n_refl,
    pos_ref, occ_ref, bf_ref, type_ref, miller_ref, obs_ref, weight_ref, ca_ref, cb_ref, cc_ref,
    grad_ref, resid_ref,
    tx, ty, tz, store, form_rows, rows, idx_v, hs, ks, ls, folds, pairs, part, reduced, mine, total_in, every, plain,
    bu, bv, bh, bk, bl,
    g_send, g_recv, r_send, r_recv, a_send, a_recv, e_send, e_recv, i_sem, j_sem,
):
    me_a = lax.axis_index("atom")
    me_r = lax.axis_index("refl")
    tiles = occ_ref.shape[0]
    refl = n_refl * LANES
    half = LANES // 2
    picks = (hs, ks, ls)

    barrier = pltpu.get_barrier_semaphore()

    def greet(s, _):
        pl.semaphore_signal(barrier, inc=1, device_id=(me_a, lax.rem(me_r + s, n_refl)), device_id_type=MESH)
        return 0

    def greet_a(s, _):
        pl.semaphore_signal(barrier, inc=1, device_id=(lax.rem(me_a + s, n_atom), me_r), device_id_type=MESH)
        return 0

    lax.fori_loop(1, n_refl, greet, 0)
    lax.fori_loop(1, n_atom, greet_a, 0)

    rows[me_r] = miller_ref[...] + top
    own_rows = pl.ds(pl.multiple_of(me_r * LANES, LANES), LANES)
    own_idx = [pltpu.make_async_copy(rows.at[me_r, d], picks[d].at[own_rows], j_sem.at[d]) for d in range(3)]
    for copy in own_idx:
        copy.start()

    pl.semaphore_wait(barrier, n_refl - 1 + n_atom - 1)

    def to_refl(src, dst, send, recv, peer):
        return pltpu.make_async_remote_copy(
            src_ref=src, dst_ref=dst, send_sem=send, recv_sem=recv,
            device_id=(me_a, peer), device_id_type=MESH,
        )

    def all_of(ref, send, recv, count):
        part_of = ref.at[pl.ds(0, count)]
        return to_refl(part_of, part_of, send, recv, me_r)

    def g_start(s, _):
        to_refl(rows.at[me_r], rows.at[me_r], g_send, g_recv, lax.rem(me_r + s, n_refl)).start()
        return 0

    lax.fori_loop(1, n_refl, g_start, 0)

    first = []
    for d in range(3):
        x = jnp.concatenate([pos_ref[d : d + 1, a * LANES : (a + 1) * LANES] for a in range(tiles)], axis=0)
        turn = two_pi * (x - jnp.round(x))
        first.append((jnp.cos(turn), jnp.sin(turn)))
    decay = bf_ref[...] * (-0.25 / (cell_edge * cell_edge))
    occ = occ_ref[...]

    def table_step(m, carry):
        mf = m.astype(jnp.float32)
        damp = jnp.exp(decay * (mf * mf))
        after = []
        for d, table in enumerate((tx, ty, tz)):
            c, s = carry[2 * d], carry[2 * d + 1]
            scale = damp * occ if d == 2 else damp
            table[top + m, 0] = c * scale
            table[top + m, 1] = s * scale
            table[top - m, 0] = c * scale
            table[top - m, 1] = -(s * scale)
            after += list(rotate(c, s, *first[d]))
        return tuple(after)

    one = jnp.ones((tiles, LANES), jnp.float32)
    zero = jnp.zeros((tiles, LANES), jnp.float32)
    lax.fori_loop(0, top + 1, table_step, (one, zero) * 3)

    kind_row = lax.broadcasted_iota(jnp.int32, (TYPES, LANES), 0)

    def column(values):
        out = jnp.full((TYPES, LANES), values[0], jnp.float32)
        for t in range(1, TYPES):
            out = jnp.where(kind_row == t, values[t], out)
        return out

    size = [column([ca_ref[g, t] for t in range(TYPES)]) for g in range(GAUSS)]
    width = [column([-0.25 * cb_ref[g, t] for t in range(TYPES)]) for g in range(GAUSS)]
    level = column([cc_ref[t] for t in range(TYPES)])
    pad = jnp.zeros((LANES - TYPES, LANES), jnp.float32)

    def forms(b, where):
        s2 = jnp.zeros((TYPES, LANES), jnp.float32)
        for d in range(3):
            m = (jnp.broadcast_to(rows[b, d : d + 1, :], (TYPES, LANES)) - top).astype(jnp.float32)
            s2 = s2 + m * m
        s2 = s2 / (cell_edge * cell_edge)
        form = size[0] * jnp.exp(width[0] * s2)
        for g in range(1, GAUSS):
            form = form + size[g] * jnp.exp(width[g] * s2)
        form_rows[where, :] = jnp.concatenate([form + level, pad], axis=0).T

    forms(me_r, own_rows)
    folds[...] = jnp.zeros_like(folds)
    for copy in own_idx:
        copy.wait()

    kind = [type_ref[v * 8 : (v + 1) * 8, :] for v in range(tiles // 8)]

    def fold():
        for j in range(2):
            for g in range(half // 4):
                at = j * half * 8 + g * 32
                q = [folds[pl.ds(at + n, 8, stride=4), :] for n in range(4)]
                pairs[(j * half + g * 4) * 2 : (j * half + g * 4) * 2 + 8, :] = (q[0] + q[1]) + (q[2] + q[3])
        wide = [pairs[pl.ds(g * 16, 8, stride=2), :] + pairs[pl.ds(g * 16 + 1, 8, stride=2), :] for g in range(LANES // 8)]
        return jnp.sum(jnp.concatenate(wide, axis=0).T, axis=0, keepdims=True)

    def block_of(step):
        return lax.rem(me_r + n_refl - step, n_refl)

    def send_part(step):
        b = block_of(step)
        to_refl(part.at[b], reduced.at[me_r], r_send, r_recv, b).start()

    def chunk(n, _):
        @pl.when(n == 2)
        def _():
            all_of(rows, g_send, g_recv, n_refl - 1).wait_recv()
            for b in range(n_refl):
                for d in range(3):
                    idx_v[d, :, b * LANES : (b + 1) * LANES] = rows[b, d : d + 1, :]
            copies = [pltpu.make_async_copy(idx_v.at[d, 0], picks[d], i_sem.at[d]) for d in range(3)]
            for copy in copies:
                copy.start()
            for b in range(n_refl):
                forms(b, pl.ds(b * LANES, LANES))
            for copy in copies:
                copy.wait()

        part[block_of(lax.div(n + 1, 2) - 1), pl.ds(lax.rem(n + 1, 2), 1), :] = fold()
        r0 = block_of(lax.div(n, 2)) * LANES + lax.rem(n, 2) * half
        for u in range(half):
            r = r0 + u
            h, k, l = hs[r], ks[r], ls[r]
            form_row = jnp.broadcast_to(form_rows[pl.ds(r, 1), :], (8, LANES))
            real, imag = None, None
            for v in range(tiles // 8):
                off = v * 8
                c, s = rotate(
                    tx[h, 0, off : off + 8, :], tx[h, 1, off : off + 8, :],
                    ty[k, 0, off : off + 8, :], ty[k, 1, off : off + 8, :],
                )
                c, s = rotate(c, s, tz[l, 0, off : off + 8, :], tz[l, 1, off : off + 8, :])
                form = jnp.take_along_axis(form_row, kind[v], axis=1, mode="promise_in_bounds")
                c = c * form
                s = s * form
                store[r, 0, off : off + 8, :] = c
                store[r, 1, off : off + 8, :] = s
                real = c if real is None else real + c
                imag = s if imag is None else imag + s
            folds[u * 8 : u * 8 + 8, :] = real
            folds[(half + u) * 8 : (half + u) * 8 + 8, :] = imag

        @pl.when(jnp.logical_and(lax.rem(n, 2) == 0, n >= 4))
        def _():
            send_part(lax.div(n, 2) - 1)

        return 0

    lax.fori_loop(0, 2 * n_refl, chunk, 0)
    part[block_of(n_refl - 1), 1:2, :] = fold()
    send_part(n_refl - 1)
    reduced[me_r] = part[me_r]

    all_of(reduced, r_send, r_recv, n_refl - 1).wait_recv()
    mine[...] = jnp.sum(reduced[...], axis=0)
    total_in[me_a] = mine[...]

    def to_atom(src, dst, peer):
        return pltpu.make_async_remote_copy(
            src_ref=src, dst_ref=dst, send_sem=a_send, recv_sem=a_recv,
            device_id=(peer, me_r), device_id_type=MESH,
        )

    def a_start(s, _):
        to_atom(mine, total_in.at[me_a], lax.rem(me_a + s, n_atom)).start()
        return 0

    lax.fori_loop(1, n_atom, a_start, 0)

    for b in range(n_refl):
        for d, wide in enumerate((bh, bk, bl)):
            m = (rows[b, d : d + 1, :] - top).astype(jnp.float32)
            wide[b * LANES : (b + 1) * LANES, :] = jnp.broadcast_to(m, (LANES, LANES)).T

    rest_a = total_in.at[pl.ds(0, n_atom - 1)]
    to_atom(rest_a, rest_a, me_a).wait_recv()
    every[me_r, 0:2, :] = jnp.sum(total_in[...], axis=0)
    every[me_r, 2:3, :] = obs_ref[...]
    every[me_r, 3:4, :] = weight_ref[...]

    def e_start(s, _):
        to_refl(every.at[me_r], every.at[me_r], e_send, e_recv, lax.rem(me_r + s, n_refl)).start()
        return 0

    lax.fori_loop(1, n_refl, e_start, 0)
    all_of(every, e_send, e_recv, n_refl - 1).wait_recv()
    for b in range(n_refl):
        for q in range(4):
            plain[q * n_refl + b : q * n_refl + b + 1, :] = every[b, q : q + 1, :]
    first_half, second_half, obs, weight = (plain[q * n_refl : (q + 1) * n_refl, :] for q in range(4))

    atoms = tiles * LANES * n_atom * n_refl
    inv_atoms = 1.0 / math.sqrt(atoms)
    low = lax.broadcasted_iota(jnp.int32, (n_refl, LANES), 1) < half
    real_part = jnp.where(low, first_half, pltpu.roll(second_half, half, 1)) * inv_atoms
    imag_part = jnp.where(low, pltpu.roll(first_half, half, 1), second_half) * inv_atoms
    amp = jnp.sqrt(real_part * real_part + imag_part * imag_part + 0.25)
    over = jnp.sum(weight * obs * amp, axis=(0, 1), keepdims=True)
    under = jnp.sum(weight * amp * amp, axis=(0, 1), keepdims=True)
    scale = over / under
    resid = scale * amp - obs
    coeff = 2.0 * weight * scale * resid / (amp * math.sqrt(refl)) * (two_pi * inv_atoms)
    along_b = coeff * imag_part
    along_a = coeff * real_part
    plain[0:n_refl, :] = resid
    resid_ref[...] = plain[pl.ds(me_r, 1), :]
    for b in range(n_refl):
        bu[b * LANES : (b + 1) * LANES, :] = jnp.broadcast_to(along_b[b : b + 1, :], (LANES, LANES)).T
        bv[b * LANES : (b + 1) * LANES, :] = jnp.broadcast_to(along_a[b : b + 1, :], (LANES, LANES)).T

    def backward_chunk(i, acc):
        acc = [list(a) for a in acc]
        r0 = pl.multiple_of(i * unroll_b, unroll_b)
        for u in range(unroll_b):
            r = r0 + u
            wide = [jnp.broadcast_to(w[pl.ds(r, 1), :], (8, LANES)) for w in (bu, bv, bh, bk, bl)]
            for v in range(tiles // 8):
                off = v * 8
                inner = wide[0] * store[r, 0, off : off + 8, :] - wide[1] * store[r, 1, off : off + 8, :]
                for d in range(3):
                    acc[d][v] = acc[d][v] + wide[2 + d] * inner
        return tuple(tuple(a) for a in acc)

    none = jnp.zeros((8, LANES), jnp.float32)
    acc = lax.fori_loop(0, refl // unroll_b, backward_chunk, ((none,) * (tiles // 8),) * 3)
    for d in range(3):
        for v in range(tiles // 8):
            for a in range(8):
                t = v * 8 + a
                grad_ref[d : d + 1, t * LANES : (t + 1) * LANES] = acc[d][v][a : a + 1, :]

    all_of(rows, g_send, g_recv, n_refl - 1).wait_send()
    all_of(part, r_send, r_recv, n_refl - 1).wait_send()
    to_atom(rest_a, rest_a, me_a).wait_send()
    all_of(every, e_send, e_recv, n_refl - 1).wait_send()


def solution(mesh):
    n_atom, n_refl = mesh.shape["atom"], mesh.shape["refl"]

    def local(positions, occupancy, bfactor, atom_type, miller, observed, weight, coef_a, coef_b, coef_c):
        shard = positions.shape[1]
        tiles = shard // LANES
        refl = miller.shape[1] * n_refl
        vmem = pl.BlockSpec(memory_space=pltpu.VMEM)
        smem = pl.BlockSpec(memory_space=pltpu.SMEM)
        f32 = jnp.float32
        table = pltpu.VMEM((2 * top + 1, 2, tiles, LANES), f32)
        wide = pltpu.VMEM((refl, LANES), f32)
        pair_r = pltpu.VMEM((n_refl, 2, LANES), f32)
        smem_row = pltpu.SMEM((refl,), jnp.int32)
        dma = pltpu.SemaphoreType.DMA
        gradient, residual = pl.pallas_call(
            functools.partial(kernel, n_atom, n_refl),
            out_shape=(
                jax.ShapeDtypeStruct((3, shard), f32),
                jax.ShapeDtypeStruct((1, LANES), f32),
            ),
            in_specs=[vmem] * 7 + [smem] * 3,
            out_specs=(vmem, vmem),
            scratch_shapes=[
                table, table, table,
                pltpu.VMEM((refl, 2, tiles, LANES), f32),
                wide,
                pltpu.VMEM((n_refl, 3, LANES), jnp.int32),
                pltpu.VMEM((3, 1, refl), jnp.int32),
                smem_row, smem_row, smem_row,
                pltpu.VMEM((8 * LANES, LANES), f32),
                pltpu.VMEM((2 * LANES, LANES), f32),
                pair_r, pair_r,
                pltpu.VMEM((2, LANES), f32),
                pltpu.VMEM((n_atom, 2, LANES), f32),
                pltpu.VMEM((n_refl, 4, LANES), f32),
                pltpu.VMEM((4 * n_refl, LANES), f32),
                wide, wide, wide, wide, wide,
                dma, dma, dma, dma, dma, dma, dma, dma,
                dma((3,)), dma((3,)),
            ],
            compiler_params=pltpu.CompilerParams(
                collective_id=0, has_side_effects=True, vmem_limit_bytes=58 * 2**20
            ),
        )(
            positions,
            occupancy.reshape(tiles, LANES),
            bfactor.reshape(tiles, LANES),
            atom_type.reshape(tiles, LANES),
            miller,
            observed.reshape(1, LANES),
            weight.reshape(1, LANES),
            coef_a.T, coef_b.T, coef_c,
        )
        return gradient, residual.reshape(LANES)

    split = P(("atom", "refl"))
    return jax.shard_map(
        local,
        mesh=mesh,
        in_specs=(
            P(None, ("atom", "refl")), split, split, split,
            P(None, "refl"), P("refl"), P("refl"), P(), P(), P(),
        ),
        out_specs=(P(None, ("atom", "refl")), P("refl")),
        check_vma=False,
    )
```

time: 59.2 us -> 53.4 us (0.902)
  Pallas kernels: 54.3 us -> 50.7 us
  local copies, waits for them, and re-layouts: 3.92 us -> 1.89 us
    pallas_call x1, Pallas kernels: 54.3 us -> 50.7 us  [local(): pl.pallas_call(functools.partial(kernel, n_atom, n_refl), out_shape=(jax....]
    unnamed x10 -> x4, local copies, waits for them, and re-layouts: 3.92 us -> 1.89 us
where the time goes in v2:
time: 53.4 us; the launch traced here: 53.2 us
  Pallas kernels  50.7 us (95%)
  local copies, waits for them, and re-layouts  1.89 us (4%)
  between operations  0.65 us (1%)
    pallas_call x1, Pallas kernels, local(): pl.pallas_call(functools.partial(kernel, n_atom, n_refl), out_shape=(jax....  50.7 us
    unnamed x4, local copies, waits for them, and re-layouts  1.89 us

profile of v2, /device:TPU:1, one launch (start us, length us, event | category | flops | bytes accessed | tf_op | source)
XLA Modules:
  0.0 53.2 jit_solution(8324034271162015522)
XLA Ops:
  0.6 50.7 %shard_map.113 = (f32[3,2048]{1,0:T(4,128)}, f32[1,128]{1,0:T(1,128)}) custom-call(f32[3,2048]{1,0:T(4,128)} %pos_ref.1, f32[16,128]{1,0:T(8,128)} %bitcast.8, f32[16,128]{1,0:T(8,128)} %bitcast.9, s32[16,128]{1,0:T(8,128)} %bitcast.10, s32[3,128]{1,0:T(4,128)} %miller_ref.1, f32[1,128]{1,0:T(1,128)} %bitcast.13, f32[1,128]{1,0:T(1,128)} %bitcast.14, ...), custom_call_target="tpu_custom_call" | custom-call | tf_op jit(solution)/shard_map/pallas_call | solution.py:298
  51.3 0.0 copy-start
  51.3 1.4 %copy.14 = f32[3,2048]{1,0:T(4,128)} copy(f32[3,2048]{1,0:T(4,128)} %get-tuple-element.8) | data formatting | bytes 49152
  52.7 0.0 copy-done
  52.7 0.5 copy.15
Async XLA Ops:
  51.3 1.4 %copy-start = (f32[1,128]{1,0:T(1,128)S(1)}, f32[1,128]{1,0:T(1,128)}, u32[]{:S(2)}) copy-start(f32[1,128]{1,0:T(1,128)} %get-tuple-element.5) | copy-start | bytes 1540

commit v3 on v2

v3 whole, which is shorter than its diff:
```python
import functools
import math

import jax
import jax.numpy as jnp
from jax import lax
from jax.experimental import pallas as pl
from jax.experimental.pallas import tpu as pltpu
from jax.sharding import PartitionSpec as P

MESH = pl.DeviceIdType.MESH
two_pi = 6.283185307179586
cell_edge = 100.0
top = 48
TYPES, GAUSS = 8, 4
LANES = 128
unroll_b = 32


def rotate(ac, as_, bc, bs):
    return ac * bc - as_ * bs, ac * bs + as_ * bc


def kernel(
    n_atom, n_refl,
    pos_ref, occ_ref, bf_ref, type_ref, miller_ref, obs_ref, weight_ref, ca_ref, cb_ref, cc_ref,
    grad_ref, resid_ref,
    tx, ty, tz, store, form_rows, rows, idx_v, hs, ks, ls, folds, pairs, seen, ow, over_atom, over_refl,
    wide_a, wide_b, wide_1, wide_2, wide_h, wide_k, wide_l,
    g_send, g_recv, o_send, o_recv, a_send, a_recv, r_send, r_recv, i_sem,
):
    me_a = lax.axis_index("atom")
    me_r = lax.axis_index("refl")
    tiles = occ_ref.shape[0]
    refl = n_refl * LANES
    half = LANES // 2
    picks = (hs, ks, ls)

    barrier = pltpu.get_barrier_semaphore()

    def greet(s, _):
        pl.semaphore_signal(barrier, inc=1, device_id=(me_a, lax.rem(me_r + s, n_refl)), device_id_type=MESH)
        return 0

    def greet_a(s, _):
        pl.semaphore_signal(barrier, inc=1, device_id=(lax.rem(me_a + s, n_atom), me_r), device_id_type=MESH)
        return 0

    lax.fori_loop(1, n_refl, greet, 0)
    lax.fori_loop(1, n_atom, greet_a, 0)

    rows[me_r] = miller_ref[...] + top
    ow[me_r, 0:1, :] = obs_ref[...]
    ow[me_r, 1:2, :] = weight_ref[...]

    pl.semaphore_wait(barrier, n_refl - 1 + n_atom - 1)

    def to_refl(src, dst, send, recv, peer):
        return pltpu.make_async_remote_copy(
            src_ref=src, dst_ref=dst, send_sem=send, recv_sem=recv,
            device_id=(me_a, peer), device_id_type=MESH,
        )

    def all_of(ref, send, recv, count):
        part_of = ref.at[pl.ds(0, count)]
        return to_refl(part_of, part_of, send, recv, me_r)

    def g_start(s, _):
        to_refl(rows.at[me_r], rows.at[me_r], g_send, g_recv, lax.rem(me_r + s, n_refl)).start()
        return 0

    def o_start(s, _):
        to_refl(ow.at[me_r], ow.at[me_r], o_send, o_recv, lax.rem(me_r + s, n_refl)).start()
        return 0

    lax.fori_loop(1, n_refl, g_start, 0)
    lax.fori_loop(1, n_refl, o_start, 0)

    first = []
    for d in range(3):
        x = jnp.concatenate([pos_ref[d : d + 1, a * LANES : (a + 1) * LANES] for a in range(tiles)], axis=0)
        turn = two_pi * (x - jnp.round(x))
        first.append((jnp.cos(turn), jnp.sin(turn)))
    decay = bf_ref[...] * (-0.25 / (cell_edge * cell_edge))
    occ = occ_ref[...]

    def table_step(m, carry):
        mf = m.astype(jnp.float32)
        damp = jnp.exp(decay * (mf * mf))
        after = []
        for d, table in enumerate((tx, ty, tz)):
            c, s = carry[2 * d], carry[2 * d + 1]
            scale = damp * occ if d == 2 else damp
            table[top + m, 0] = c * scale
            table[top + m, 1] = s * scale
            table[top - m, 0] = c * scale
            table[top - m, 1] = -(s * scale)
            after += list(rotate(c, s, *first[d]))
        return tuple(after)

    one = jnp.ones((tiles, LANES), jnp.float32)
    zero = jnp.zeros((tiles, LANES), jnp.float32)
    lax.fori_loop(0, top + 1, table_step, (one, zero) * 3)

    kind_row = lax.broadcasted_iota(jnp.int32, (TYPES, LANES), 0)

    def column(values):
        out = jnp.full((TYPES, LANES), values[0], jnp.float32)
        for t in range(1, TYPES):
            out = jnp.where(kind_row == t, values[t], out)
        return out

    size = [column([ca_ref[g, t] for t in range(TYPES)]) for g in range(GAUSS)]
    width = [column([-0.25 * cb_ref[g, t] for t in range(TYPES)]) for g in range(GAUSS)]
    level = column([cc_ref[t] for t in range(TYPES)])
    pad = jnp.zeros((LANES - TYPES, LANES), jnp.float32)

    def forms(b, where):
        s2 = jnp.zeros((TYPES, LANES), jnp.float32)
        for d in range(3):
            m = (jnp.broadcast_to(rows[b, d : d + 1, :], (TYPES, LANES)) - top).astype(jnp.float32)
            s2 = s2 + m * m
        s2 = s2 / (cell_edge * cell_edge)
        form = size[0] * jnp.exp(width[0] * s2)
        for g in range(1, GAUSS):
            form = form + size[g] * jnp.exp(width[g] * s2)
        form_rows[where, :] = jnp.concatenate([form + level, pad], axis=0).T

    folds[...] = jnp.zeros_like(folds)
    kind = [type_ref[v * 8 : (v + 1) * 8, :] for v in range(tiles // 8)]

    ones = jnp.ones((8, LANES), jnp.bfloat16)

    def fold():
        for j in range(2):
            for g in range(half // 4):
                at = j * half * 8 + g * 32
                q = [folds[pl.ds(at + n, 8, stride=4), :] for n in range(4)]
                pairs[(j * half + g * 4) * 2 : (j * half + g * 4) * 2 + 8, :] = (q[0] + q[1]) + (q[2] + q[3])
        wide = [pairs[pl.ds(g * 16, 8, stride=2), :] + pairs[pl.ds(g * 16 + 1, 8, stride=2), :] for g in range(LANES // 8)]
        wide = jnp.concatenate(wide, axis=0)
        high = wide.astype(jnp.bfloat16)
        rest = (wide - high.astype(jnp.float32)).astype(jnp.bfloat16)
        lanes = (((1,), (1,)), ((), ()))
        total = lax.dot_general(ones, high, lanes, preferred_element_type=jnp.float32) + lax.dot_general(
            ones, rest, lanes, preferred_element_type=jnp.float32
        )
        return total[0:1, :]

    all_of(rows, g_send, g_recv, n_refl - 1).wait_recv()
    for b in range(n_refl):
        for d in range(3):
            idx_v[d, :, b * LANES : (b + 1) * LANES] = rows[b, d : d + 1, :]
    copies = [pltpu.make_async_copy(idx_v.at[d, 0], picks[d], i_sem.at[d]) for d in range(3)]
    for copy in copies:
        copy.start()
    for b in range(n_refl):
        forms(b, pl.ds(b * LANES, LANES))
    for copy in copies:
        copy.wait()

    steps = 2 * n_refl
    per = 8
    chunks = steps // per

    def to_atom(src, dst, q, peer):
        return pltpu.make_async_remote_copy(
            src_ref=src, dst_ref=dst, send_sem=a_send.at[q], recv_sem=a_recv.at[q],
            device_id=(peer, me_r), device_id_type=MESH,
        )

    def rest_atom(q):
        part_of = over_atom.at[q, pl.ds(0, n_atom - 1)]
        return to_atom(part_of, part_of, q, me_a)

    def rest_refl(q):
        part_of = over_refl.at[q, pl.ds(0, n_refl - 1)]
        return to_refl(part_of, part_of, r_send.at[q], r_recv.at[q], me_r)

    def send_atom(q):
        def one(s, _):
            mine = over_atom.at[q, me_a]
            to_atom(mine, mine, q, lax.rem(me_a + s, n_atom)).start()
            return 0

        lax.fori_loop(1, n_atom, one, 0)

    def send_refl(q):
        rest_atom(q).wait_recv()
        over_refl[q, me_r] = jnp.sum(over_atom[q], axis=0)

        def one(s, _):
            mine = over_refl.at[q, me_r]
            to_refl(mine, mine, r_send.at[q], r_recv.at[q], lax.rem(me_r + s, n_refl)).start()
            return 0

        lax.fori_loop(1, n_refl, one, 0)

    def forward_step(n, _):
        before = lax.rem(n + steps - 1, steps)
        over_atom[lax.div(before, per), me_a, pl.ds(lax.rem(before, per), 1), :] = fold()
        r0 = n * half
        for u in range(half):
            r = r0 + u
            h, k, l = hs[r], ks[r], ls[r]
            form_row = jnp.broadcast_to(form_rows[pl.ds(r, 1), :], (8, LANES))
            real, imag = None, None
            for v in range(tiles // 8):
                off = v * 8
                c, s = rotate(
                    tx[h, 0, off : off + 8, :], tx[h, 1, off : off + 8, :],
                    ty[k, 0, off : off + 8, :], ty[k, 1, off : off + 8, :],
                )
                c, s = rotate(c, s, tz[l, 0, off : off + 8, :], tz[l, 1, off : off + 8, :])
                form = jnp.take_along_axis(form_row, kind[v], axis=1, mode="promise_in_bounds")
                c = c * form
                s = s * form
                store[r, 0, off : off + 8, :] = c
                store[r, 1, off : off + 8, :] = s
                real = c if real is None else real + c
                imag = s if imag is None else imag + s
            folds[u * 8 : u * 8 + 8, :] = real
            folds[(half + u) * 8 : (half + u) * 8 + 8, :] = imag

        @pl.when(jnp.logical_and(lax.rem(n, per) == 0, n >= per))
        def _():
            send_atom(lax.div(n, per) - 1)

        return 0

    lax.fori_loop(0, steps, forward_step, 0)
    over_atom[chunks - 1, me_a, per - 1 : per, :] = fold()
    send_atom(chunks - 1)

    atoms = tiles * LANES * n_atom * n_refl
    inv_atoms = 1.0 / math.sqrt(atoms)
    factor = 2.0 / math.sqrt(refl)
    low = lax.broadcasted_iota(jnp.int32, (per, LANES), 1) < half

    def spread(row):
        return jnp.broadcast_to(row, (LANES, LANES)).T

    all_of(ow, o_send, o_recv, n_refl - 1).wait_recv()
    low_row = lax.broadcasted_iota(jnp.int32, (1, LANES), 1) < half
    for b in range(n_refl):
        for q in range(2):
            row = ow[b, q : q + 1, :]
            turned = pltpu.roll(row, half, 1)
            seen[q, 2 * b : 2 * b + 1, :] = jnp.where(low_row, row, turned)
            seen[q, 2 * b + 1 : 2 * b + 2, :] = jnp.where(low_row, turned, row)

    send_refl(0)
    for b in range(n_refl):
        for d, wide in enumerate((wide_h, wide_k, wide_l)):
            wide[b * LANES : (b + 1) * LANES, :] = spread((rows[b, d : d + 1, :] - top).astype(jnp.float32))
    send_refl(1)
    send_refl(2)

    def totals(q):
        rest_refl(q).wait_recv()
        both = jnp.sum(over_refl[q], axis=0) * inv_atoms
        square = both * both
        amp = jnp.sqrt(square + pltpu.roll(square, half, 1) + 0.25)
        return both, amp, seen[0, q * per : (q + 1) * per, :], seen[1, q * per : (q + 1) * per, :]

    def place(q, values, first, second):
        for i in range(per):
            at = (q * per + i) * half
            block = spread(values[i : i + 1, :])
            first[at : at + half, :] = block[:half]
            second[at : at + half, :] = block[half:]

    def both_sums(q, both, amp, obs, weight):
        place(q, both, wide_a, wide_b)
        place(q, jnp.where(low, factor * weight, factor * weight * obs / amp), wide_1, wide_2)

    def wide_rows(r, sources):
        return [jnp.broadcast_to(w[pl.ds(r, 1), :], (8, LANES)) for w in sources]

    def early(i, acc):
        acc = [[list(a) for a in g] for g in acc]
        r0 = i * unroll_b
        for u in range(unroll_b):
            r = r0 + u
            a, b, w1, w2, *m = wide_rows(r, (wide_a, wide_b, wide_1, wide_2, wide_h, wide_k, wide_l))
            for v in range(tiles // 8):
                off = v * 8
                p = b * store[r, 0, off : off + 8, :] - a * store[r, 1, off : off + 8, :]
                for g, w in enumerate((w1, w2)):
                    inner = w * p
                    for d in range(3):
                        acc[g][d][v] = acc[g][d][v] + m[d] * inner
        return tuple(tuple(tuple(a) for a in g) for g in acc)

    def late(i, acc):
        acc = [list(a) for a in acc]
        r0 = i * unroll_b
        for u in range(unroll_b):
            r = r0 + u
            a, b, *m = wide_rows(r, (wide_a, wide_b, wide_h, wide_k, wide_l))
            for v in range(tiles // 8):
                off = v * 8
                inner = b * store[r, 0, off : off + 8, :] - a * store[r, 1, off : off + 8, :]
                for d in range(3):
                    acc[d][v] = acc[d][v] + m[d] * inner
        return tuple(tuple(a) for a in acc)

    none = jnp.zeros((8, LANES), jnp.float32)
    group = ((none,) * (tiles // 8),) * 3
    size_q = per * half // unroll_b
    known = [totals(0)]
    both_sums(0, *known[0])
    acc2 = lax.fori_loop(0, size_q // 2, early, (group, group))
    send_refl(3)
    acc2 = lax.fori_loop(size_q // 2, size_q, early, acc2)
    known.append(totals(1))
    both_sums(1, *known[1])
    acc2 = lax.fori_loop(size_q, 2 * size_q, early, acc2)
    known += [totals(q) for q in range(2, chunks)]

    over = sum(jnp.where(low, weight * obs * amp, 0.0) for _, amp, obs, weight in known)
    under = sum(jnp.where(low, weight * amp * amp, 0.0) for _, amp, obs, weight in known)
    over = jnp.sum(over, axis=(0, 1), keepdims=True)
    under = jnp.sum(under, axis=(0, 1), keepdims=True)
    scale = over / under
    for q, (both, amp, obs, weight) in enumerate(known):
        seen[0, q * per : (q + 1) * per, :] = scale * amp
        if q >= 2:
            place(q, factor * weight * scale * (scale * amp - obs) / amp * both, wide_a, wide_b)
    acc = lax.fori_loop(2 * size_q, chunks * size_q, late, group)
    for d in range(3):
        for v in range(tiles // 8):
            total = acc[d][v] + scale * (scale * acc2[0][d][v] - acc2[1][d][v])
            for a in range(8):
                t = v * 8 + a
                grad_ref[d : d + 1, t * LANES : (t + 1) * LANES] = total[a : a + 1, :]
    resid_ref[...] = jnp.where(low_row, seen[0, pl.ds(2 * me_r, 1), :], seen[0, pl.ds(2 * me_r + 1, 1), :])

    all_of(rows, g_send, g_recv, n_refl - 1).wait_send()
    all_of(ow, o_send, o_recv, n_refl - 1).wait_send()
    for q in range(chunks):
        rest_atom(q).wait_send()
        rest_refl(q).wait_send()


def solution(mesh):
    n_atom, n_refl = mesh.shape["atom"], mesh.shape["refl"]

    def local(positions, occupancy, bfactor, atom_type, miller, observed, weight, coef_a, coef_b, coef_c):
        shard = positions.shape[1]
        tiles = shard // LANES
        refl = miller.shape[1] * n_refl
        vmem = pl.BlockSpec(memory_space=pltpu.VMEM)
        smem = pl.BlockSpec(memory_space=pltpu.SMEM)
        f32 = jnp.float32
        table = pltpu.VMEM((2 * top + 1, 2, tiles, LANES), f32)
        wide = pltpu.VMEM((refl, LANES), f32)
        smem_row = pltpu.SMEM((refl,), jnp.int32)
        dma = pltpu.SemaphoreType.DMA
        chunks = 2 * n_refl // 8
        gradient, residual = pl.pallas_call(
            functools.partial(kernel, n_atom, n_refl),
            out_shape=(
                jax.ShapeDtypeStruct((3, shard), f32),
                jax.ShapeDtypeStruct((1, LANES), f32),
            ),
            in_specs=[vmem] * 7 + [smem] * 3,
            out_specs=(vmem, vmem),
            scratch_shapes=[
                table, table, table,
                pltpu.VMEM((refl, 2, tiles, LANES), f32),
                wide,
                pltpu.VMEM((n_refl, 3, LANES), jnp.int32),
                pltpu.VMEM((3, 1, refl), jnp.int32),
                smem_row, smem_row, smem_row,
                pltpu.VMEM((8 * LANES, LANES), f32),
                pltpu.VMEM((2 * LANES, LANES), f32),
                pltpu.VMEM((2, 2 * n_refl, LANES), f32),
                pltpu.VMEM((n_refl, 2, LANES), f32),
                pltpu.VMEM((chunks, n_atom, 8, LANES), f32),
                pltpu.VMEM((chunks, n_refl, 8, LANES), f32),
                wide, wide, wide, wide, wide, wide, wide,
                dma, dma, dma, dma,
                dma((chunks,)), dma((chunks,)), dma((chunks,)), dma((chunks,)),
                dma((3,)),
            ],
            compiler_params=pltpu.CompilerParams(
                collective_id=0, has_side_effects=True, vmem_limit_bytes=58 * 2**20
            ),
        )(
            positions,
            occupancy.reshape(tiles, LANES),
            bfactor.reshape(tiles, LANES),
            atom_type.reshape(tiles, LANES),
            miller,
            observed.reshape(1, LANES),
            weight.reshape(1, LANES),
            coef_a.T, coef_b.T, coef_c,
        )
        inv_atoms = 1.0 / math.sqrt(shard * n_atom * n_refl)
        return gradient * (two_pi * inv_atoms), residual.reshape(LANES) - observed

    split = P(("atom", "refl"))
    return jax.shard_map(
        local,
        mesh=mesh,
        in_specs=(
            P(None, ("atom", "refl")), split, split, split,
            P(None, "refl"), P("refl"), P("refl"), P(), P(), P(),
        ),
        out_specs=(P(None, ("atom", "refl")), P("refl")),
        check_vma=False,
    )
```

time: 53.4 us -> 49.2 us (0.921)
  the two profiles are of different devices: /device:TPU:1 before, /device:TPU:8 now
where the time goes in v3:
time: 49.2 us; the launch traced here: 49 us
  Pallas kernels  46.4 us (94%)
  other arithmetic  1.9 us (4%)
  between operations  0.66 us (1%)
    pallas_call x1, Pallas kernels, local(): pl.pallas_call(functools.partial(kernel, n_atom, n_refl), out_shape=(jax....  46.4 us
    mul x1, other arithmetic, local(): return (gradient * (two_pi * inv_atoms), residual.reshape(LANES) - observed)  1.38 us

profile of v3, /device:TPU:8, one launch (start us, length us, event | category | flops | bytes accessed | tf_op | source)
XLA Modules:
  0.0 49.0 jit_solution(2668165936018441694)
XLA Ops:
  0.6 46.4 %shard_map.113 = (f32[3,2048]{1,0:T(4,128)}, f32[1,128]{1,0:T(1,128)}) custom-call(f32[3,2048]{1,0:T(4,128)} %pos_ref.1, f32[16,128]{1,0:T(8,128)} %bitcast.9, f32[16,128]{1,0:T(8,128)} %bitcast.10, s32[16,128]{1,0:T(8,128)} %bitcast.11, s32[3,128]{1,0:T(4,128)} %miller_ref.1, f32[1,128]{1,0:T(1,128)} %bitcast.15, f32[1,128]{1,0:T(1,128)} %bitcast.14, ...), custom_call_target="tpu_custom_call" | custom-call | tf_op jit(solution)/shard_map/pallas_call | solution.py:361
  47.1 0.0 copy-start
  47.1 0.0 copy-start.1
  47.1 1.4 %broadcast_multiply_fusion = f32[3,2048]{1,0:T(4,128)} fusion(f32[3,2048]{1,0:T(4,128)} %get-tuple-element.4), kind=kLoop, calls=%fused_computation | loop fusion | flops 6144 | bytes 49152 | tf_op jit(solution)/shard_map/mul | solution.py:401
  48.5 0.0 copy-done
  48.5 0.0 copy-done.1
  48.5 0.5 %bitcast_subtract_fusion = f32[128]{0:T(128)} fusion(f32[128]{0:T(128)S(1)} %copy-done, f32[1,128]{1,0:T(1,128)S(1)} %copy-done.1), kind=kLoop, calls=%fused_computation.1 | loop fusion | flops 128 | bytes 1536 | tf_op jit(solution)/shard_map/sub | solution.py:401
Async XLA Ops:
  47.1 1.4 %copy-start = (f32[128]{0:T(128)S(1)}, f32[128]{0:T(128)}, u32[]{:S(2)}) copy-start(f32[128]{0:T(128)} %param.15) | copy-start | bytes 1540
  47.1 1.4 %copy-start.1 = (f32[1,128]{1,0:T(1,128)S(1)}, f32[1,128]{1,0:T(1,128)}, u32[]{:S(2)}) copy-start(f32[1,128]{1,0:T(1,128)} %get-tuple-element.5) | copy-start | bytes 1540

commit v4 on v3

--- a/solution.py
+++ b/solution.py
@@ -14,6 +14,7 @@
 top = 48
 TYPES, GAUSS = 8, 4
 LANES = 128
+SIDE = 4
 unroll_b = 32
 
 
@@ -25,9 +26,9 @@
     n_atom, n_refl,
     pos_ref, occ_ref, bf_ref, type_ref, miller_ref, obs_ref, weight_ref, ca_ref, cb_ref, cc_ref,
     grad_ref, resid_ref,
-    tx, ty, tz, store, form_rows, rows, idx_v, hs, ks, ls, folds, pairs, seen, ow, over_atom, over_refl,
+    tx, ty, tz, store, form_rows, rows, idx_v, hs, ks, ls, folds, pairs, seen, ow, in_column, in_plane,
     wide_a, wide_b, wide_1, wide_2, wide_h, wide_k, wide_l,
-    g_send, g_recv, o_send, o_recv, a_send, a_recv, r_send, r_recv, i_sem,
+    g_send, g_recv, o_send, o_recv, c_send, c_recv, p_send, p_recv, i_sem, j_sem,
 ):
     me_a = lax.axis_index("atom")
     me_r = lax.axis_index("refl")
@@ -36,24 +37,45 @@
     half = LANES // 2
     picks = (hs, ks, ls)
 
+    x, zc = lax.div(me_a, SIDE), lax.rem(me_a, SIDE)
+    z, y = lax.div(me_r, SIDE), lax.rem(me_r, SIDE)
+    column = z * SIDE + zc
+    plane = x * SIDE + y
+
+    def column_peer(slot):
+        return x * SIDE + lax.rem(slot, SIDE), lax.div(slot, SIDE) * SIDE + y
+
+    def plane_peer(slot):
+        return lax.div(slot, SIDE) * SIDE + zc, z * SIDE + lax.rem(slot, SIDE)
+
     barrier = pltpu.get_barrier_semaphore()
 
-    def greet(s, _):
-        pl.semaphore_signal(barrier, inc=1, device_id=(me_a, lax.rem(me_r + s, n_refl)), device_id_type=MESH)
+    def greet(peer):
+        pl.semaphore_signal(barrier, inc=1, device_id=peer, device_id_type=MESH)
+
+    def greet_far(i, _):
+        turn, other = 1 + lax.div(i, SIDE), lax.rem(i, SIDE)
+        greet(column_peer(other * SIDE + lax.rem(zc + turn, SIDE)))
+        greet(plane_peer(lax.rem(x + turn, SIDE) * SIDE + other))
         return 0
 
-    def greet_a(s, _):
-        pl.semaphore_signal(barrier, inc=1, device_id=(lax.rem(me_a + s, n_atom), me_r), device_id_type=MESH)
+    def greet_refl(s, _):
+        greet((me_a, lax.rem(me_r + s, n_refl)))
         return 0
 
-    lax.fori_loop(1, n_refl, greet, 0)
-    lax.fori_loop(1, n_atom, greet_a, 0)
+    far = SIDE * (SIDE - 1)
+    lax.fori_loop(0, far, greet_far, 0)
+    lax.fori_loop(1, n_refl, greet_refl, 0)
 
     rows[me_r] = miller_ref[...] + top
     ow[me_r, 0:1, :] = obs_ref[...]
     ow[me_r, 1:2, :] = weight_ref[...]
-
-    pl.semaphore_wait(barrier, n_refl - 1 + n_atom - 1)
+    own_rows = pl.ds(pl.multiple_of(me_r * LANES, LANES), LANES)
+    own_idx = [pltpu.make_async_copy(rows.at[me_r, d], picks[d].at[own_rows], j_sem.at[d]) for d in range(3)]
+    for copy in own_idx:
+        copy.start()
+
+    pl.semaphore_wait(barrier, n_refl - 1 + 2 * far)
 
     def to_refl(src, dst, send, recv, peer):
         return pltpu.make_async_remote_copy(
@@ -78,8 +100,8 @@
 
     first = []
     for d in range(3):
-        x = jnp.concatenate([pos_ref[d : d + 1, a * LANES : (a + 1) * LANES] for a in range(tiles)], axis=0)
-        turn = two_pi * (x - jnp.round(x))
+        coord = jnp.concatenate([pos_ref[d : d + 1, a * LANES : (a + 1) * LANES] for a in range(tiles)], axis=0)
+        turn = two_pi * (coord - jnp.round(coord))
         first.append((jnp.cos(turn), jnp.sin(turn)))
     decay = bf_ref[...] * (-0.25 / (cell_edge * cell_edge))
     occ = occ_ref[...]
@@ -104,15 +126,15 @@
 
     kind_row = lax.broadcasted_iota(jnp.int32, (TYPES, LANES), 0)
 
-    def column(values):
+    def by_type(values):
         out = jnp.full((TYPES, LANES), values[0], jnp.float32)
         for t in range(1, TYPES):
             out = jnp.where(kind_row == t, values[t], out)
         return out
 
-    size = [column([ca_ref[g, t] for t in range(TYPES)]) for g in range(GAUSS)]
-    width = [column([-0.25 * cb_ref[g, t] for t in range(TYPES)]) for g in range(GAUSS)]
-    level = column([cc_ref[t] for t in range(TYPES)])
+    size = [by_type([ca_ref[g, t] for t in range(TYPES)]) for g in range(GAUSS)]
+    width = [by_type([-0.25 * cb_ref[g, t] for t in range(TYPES)]) for g in range(GAUSS)]
+    level = by_type([cc_ref[t] for t in range(TYPES)])
     pad = jnp.zeros((LANES - TYPES, LANES), jnp.float32)
 
     def forms(b, where):
@@ -126,7 +148,10 @@
             form = form + size[g] * jnp.exp(width[g] * s2)
         form_rows[where, :] = jnp.concatenate([form + level, pad], axis=0).T
 
+    forms(me_r, own_rows)
     folds[...] = jnp.zeros_like(folds)
+    for copy in own_idx:
+        copy.wait()
     kind = [type_ref[v * 8 : (v + 1) * 8, :] for v in range(tiles // 8)]
 
     ones = jnp.ones((8, LANES), jnp.bfloat16)
@@ -147,58 +172,72 @@
         )
         return total[0:1, :]
 
-    all_of(rows, g_send, g_recv, n_refl - 1).wait_recv()
-    for b in range(n_refl):
-        for d in range(3):
-            idx_v[d, :, b * LANES : (b + 1) * LANES] = rows[b, d : d + 1, :]
-    copies = [pltpu.make_async_copy(idx_v.at[d, 0], picks[d], i_sem.at[d]) for d in range(3)]
-    for copy in copies:
-        copy.start()
-    for b in range(n_refl):
-        forms(b, pl.ds(b * LANES, LANES))
-    for copy in copies:
-        copy.wait()
-
     steps = 2 * n_refl
     per = 8
     chunks = steps // per
 
-    def to_atom(src, dst, q, peer):
+    def to_column(src, q, slot):
         return pltpu.make_async_remote_copy(
-            src_ref=src, dst_ref=dst, send_sem=a_send.at[q], recv_sem=a_recv.at[q],
-            device_id=(peer, me_r), device_id_type=MESH,
+            src_ref=src, dst_ref=src, send_sem=c_send.at[q], recv_sem=c_recv.at[q],
+            device_id=column_peer(slot), device_id_type=MESH,
         )
 
-    def rest_atom(q):
-        part_of = over_atom.at[q, pl.ds(0, n_atom - 1)]
-        return to_atom(part_of, part_of, q, me_a)
-
-    def rest_refl(q):
-        part_of = over_refl.at[q, pl.ds(0, n_refl - 1)]
-        return to_refl(part_of, part_of, r_send.at[q], r_recv.at[q], me_r)
-
-    def send_atom(q):
+    def to_plane(src, q, slot):
+        return pltpu.make_async_remote_copy(
+            src_ref=src, dst_ref=src, send_sem=p_send.at[q], recv_sem=p_recv.at[q],
+            device_id=plane_peer(slot), device_id_type=MESH,
+        )
+
+    peers = SIDE * SIDE
+
+    def rest_column(q):
+        return to_column(in_column.at[q, pl.ds(0, peers - 1)], q, column)
+
+    def rest_plane(q):
+        return to_plane(in_plane.at[q, pl.ds(0, peers - 1)], q, plane)
+
+    def send_column(q):
         def one(s, _):
-            mine = over_atom.at[q, me_a]
-            to_atom(mine, mine, q, lax.rem(me_a + s, n_atom)).start()
+            to_column(in_column.at[q, column], q, lax.rem(column + s, peers)).start()
             return 0
 
-        lax.fori_loop(1, n_atom, one, 0)
-
-    def send_refl(q):
-        rest_atom(q).wait_recv()
-        over_refl[q, me_r] = jnp.sum(over_atom[q], axis=0)
+        lax.fori_loop(1, peers, one, 0)
+
+    def send_plane(q):
+        rest_column(q).wait_recv()
+        in_plane[q, plane] = jnp.sum(in_column[q], axis=0)
 
         def one(s, _):
-            mine = over_refl.at[q, me_r]
-            to_refl(mine, mine, r_send.at[q], r_recv.at[q], lax.rem(me_r + s, n_refl)).start()
+            to_plane(in_plane.at[q, plane], q, lax.rem(plane + s, peers)).start()
             return 0
 
-        lax.fori_loop(1, n_refl, one, 0)
-
-    def forward_step(n, _):
-        before = lax.rem(n + steps - 1, steps)
-        over_atom[lax.div(before, per), me_a, pl.ds(lax.rem(before, per), 1), :] = fold()
+        lax.fori_loop(1, peers, one, 0)
+
+    def step_at(i):
+        later = i - 2
+        return jnp.where(i < 2, 2 * me_r + i, jnp.where(later < 2 * me_r, later, i))
+
+    def prepare():
+        all_of(rows, g_send, g_recv, n_refl - 1).wait_recv()
+        for b in range(n_refl):
+            for d in range(3):
+                idx_v[d, :, b * LANES : (b + 1) * LANES] = rows[b, d : d + 1, :]
+        copies = [pltpu.make_async_copy(idx_v.at[d, 0], picks[d], i_sem.at[d]) for d in range(3)]
+        for copy in copies:
+            copy.start()
+        for b in range(n_refl):
+            forms(b, pl.ds(b * LANES, LANES))
+        for copy in copies:
+            copy.wait()
+
+    def forward_step(i, _):
+        @pl.when(i == 2)
+        def _():
+            prepare()
+
+        n = step_at(i)
+        before = step_at(lax.rem(i + steps - 1, steps))
+        in_column[lax.div(before, per), column, pl.ds(lax.rem(before, per), 1), :] = fold()
         r0 = n * half
         for u in range(half):
             r = r0 + u
@@ -222,15 +261,16 @@
             folds[u * 8 : u * 8 + 8, :] = real
             folds[(half + u) * 8 : (half + u) * 8 + 8, :] = imag
 
-        @pl.when(jnp.logical_and(lax.rem(n, per) == 0, n >= per))
+        @pl.when(jnp.logical_and(i > 2, lax.div(n, per) > lax.div(before, per)))
         def _():
-            send_atom(lax.div(n, per) - 1)
+            send_column(lax.div(before, per))
 
         return 0
 
     lax.fori_loop(0, steps, forward_step, 0)
-    over_atom[chunks - 1, me_a, per - 1 : per, :] = fold()
-    send_atom(chunks - 1)
+    last = step_at(steps - 1)
+    in_column[chunks - 1, column, pl.ds(lax.rem(last, per), 1), :] = fold()
+    send_column(chunks - 1)
 
     atoms = tiles * LANES * n_atom * n_refl
     inv_atoms = 1.0 / math.sqrt(atoms)
@@ -249,16 +289,16 @@
             seen[q, 2 * b : 2 * b + 1, :] = jnp.where(low_row, row, turned)
             seen[q, 2 * b + 1 : 2 * b + 2, :] = jnp.where(low_row, turned, row)
 
-    send_refl(0)
+    send_plane(0)
     for b in range(n_refl):
         for d, wide in enumerate((wide_h, wide_k, wide_l)):
             wide[b * LANES : (b + 1) * LANES, :] = spread((rows[b, d : d + 1, :] - top).astype(jnp.float32))
-    send_refl(1)
-    send_refl(2)
+    send_plane(1)
+    send_plane(2)
 
     def totals(q):
-        rest_refl(q).wait_recv()
-        both = jnp.sum(over_refl[q], axis=0) * inv_atoms
+        rest_plane(q).wait_recv()
+        both = jnp.sum(in_plane[q], axis=0) * inv_atoms
         square = both * both
         amp = jnp.sqrt(square + pltpu.roll(square, half, 1) + 0.25)
         return both, amp, seen[0, q * per : (q + 1) * per, :], seen[1, q * per : (q + 1) * per, :]
@@ -310,9 +350,9 @@
     size_q = per * half // unroll_b
     known = [totals(0)]
     both_sums(0, *known[0])
-    acc2 = lax.fori_loop(0, size_q // 2, early, (group, group))
-    send_refl(3)
-    acc2 = lax.fori_loop(size_q // 2, size_q, early, acc2)
+    acc2 = lax.fori_loop(0, size_q // 4, early, (group, group))
+    send_plane(3)
+    acc2 = lax.fori_loop(size_q // 4, size_q, early, acc2)
     known.append(totals(1))
     both_sums(1, *known[1])
     acc2 = lax.fori_loop(size_q, 2 * size_q, early, acc2)
@@ -339,8 +379,8 @@
     all_of(rows, g_send, g_recv, n_refl - 1).wait_send()
     all_of(ow, o_send, o_recv, n_refl - 1).wait_send()
     for q in range(chunks):
-        rest_atom(q).wait_send()
-        rest_refl(q).wait_send()
+        rest_column(q).wait_send()
+        rest_plane(q).wait_send()
 
 
 def solution(mesh):
@@ -377,12 +417,12 @@
                 pltpu.VMEM((2 * LANES, LANES), f32),
                 pltpu.VMEM((2, 2 * n_refl, LANES), f32),
                 pltpu.VMEM((n_refl, 2, LANES), f32),
-                pltpu.VMEM((chunks, n_atom, 8, LANES), f32),
-                pltpu.VMEM((chunks, n_refl, 8, LANES), f32),
+                pltpu.VMEM((chunks, SIDE * SIDE, 8, LANES), f32),
+                pltpu.VMEM((chunks, SIDE * SIDE, 8, LANES), f32),
                 wide, wide, wide, wide, wide, wide, wide,
                 dma, dma, dma, dma,
                 dma((chunks,)), dma((chunks,)), dma((chunks,)), dma((chunks,)),
-                dma((3,)),
+                dma((3,)), dma((3,)),
             ],
             compiler_params=pltpu.CompilerParams(
                 collective_id=0, has_side_effects=True, vmem_limit_bytes=58 * 2**20

time: 49.2 us -> 46.5 us (0.945)
  the two profiles are of different devices: /device:TPU:8 before, /device:TPU:1 now
where the time goes in v4:
time: 46.5 us; the launch traced here: 46.3 us
  Pallas kernels  43.7 us (94%)
  other arithmetic  1.9 us (4%)
  between operations  0.66 us (1%)
    pallas_call x1, Pallas kernels, local(): pl.pallas_call(functools.partial(kernel, n_atom, n_refl), out_shape=(jax....  43.7 us
    mul x1, other arithmetic, local(): return (gradient * (two_pi * inv_atoms), residual.reshape(LANES) - observed)  1.38 us

profile of v4, /device:TPU:1, one launch (start us, length us, event | category | flops | bytes accessed | tf_op | source)
XLA Modules:
  0.0 46.3 jit_solution(6722647737813856982)
XLA Ops:
  0.6 43.7 %shard_map.113 = (f32[3,2048]{1,0:T(4,128)}, f32[1,128]{1,0:T(1,128)}) custom-call(f32[3,2048]{1,0:T(4,128)} %pos_ref.1, f32[16,128]{1,0:T(8,128)} %bitcast.9, f32[16,128]{1,0:T(8,128)} %bitcast.10, s32[16,128]{1,0:T(8,128)} %bitcast.11, s32[3,128]{1,0:T(4,128)} %miller_ref.1, f32[1,128]{1,0:T(1,128)} %bitcast.15, f32[1,128]{1,0:T(1,128)} %bitcast.14, ...), custom_call_target="tpu_custom_call" | custom-call | tf_op jit(solution)/shard_map/pallas_call | solution.py:401
  44.4 0.0 copy-start
  44.4 0.0 copy-start.1
  44.4 1.4 %broadcast_multiply_fusion = f32[3,2048]{1,0:T(4,128)} fusion(f32[3,2048]{1,0:T(4,128)} %get-tuple-element.4), kind=kLoop, calls=%fused_computation | loop fusion | flops 6144 | bytes 49152 | tf_op jit(solution)/shard_map/mul | solution.py:441
  45.8 0.0 copy-done
  45.8 0.0 copy-done.1
  45.8 0.5 %bitcast_subtract_fusion = f32[128]{0:T(128)} fusion(f32[128]{0:T(128)S(1)} %copy-done, f32[1,128]{1,0:T(1,128)S(1)} %copy-done.1), kind=kLoop, calls=%fused_computation.1 | loop fusion | flops 128 | bytes 1536 | tf_op jit(solution)/shard_map/sub | solution.py:441
Async XLA Ops:
  44.4 1.4 %copy-start = (f32[128]{0:T(128)S(1)}, f32[128]{0:T(128)}, u32[]{:S(2)}) copy-start(f32[128]{0:T(128)} %param.15) | copy-start | bytes 1540
  44.4 1.4 %copy-start.1 = (f32[1,128]{1,0:T(1,128)S(1)}, f32[1,128]{1,0:T(1,128)}, u32[]{:S(2)}) copy-start(f32[1,128]{1,0:T(1,128)} %get-tuple-element.5) | copy-start | bytes 1540

commit v5 on v4

--- a/solution.py
+++ b/solution.py
@@ -22,14 +22,14 @@
     return ac * bc - as_ * bs, ac * bs + as_ * bc
 
 
-def kernel(
-    n_atom, n_refl,
-    pos_ref, occ_ref, bf_ref, type_ref, miller_ref, obs_ref, weight_ref, ca_ref, cb_ref, cc_ref,
-    grad_ref, resid_ref,
-    tx, ty, tz, store, form_rows, rows, idx_v, hs, ks, ls, folds, pairs, seen, ow, in_column, in_plane,
-    wide_a, wide_b, wide_1, wide_2, wide_h, wide_k, wide_l,
-    g_send, g_recv, o_send, o_recv, c_send, c_recv, p_send, p_recv, i_sem, j_sem,
-):
+def kernel(n_atom, n_refl, *refs):
+    sources, (grad_ref, resid_ref), inputs, rest = refs[:10], refs[10:12], refs[12:22], refs[22:]
+    pos_ref, occ_ref, bf_ref, type_ref, miller_ref, obs_ref, weight_ref, ca_ref, cb_ref, cc_ref = inputs
+    (
+        tx, ty, tz, store, form_rows, rows, idx_v, hs, ks, ls, folds, pairs, seen, ow, in_column, in_plane,
+        wide_a, wide_b, wide_1, wide_2, wide_h, wide_k, wide_l,
+        g_send, g_recv, o_send, o_recv, c_send, c_recv, p_send, p_recv, i_sem, j_sem, in_sem,
+    ) = rest
     me_a = lax.axis_index("atom")
     me_r = lax.axis_index("refl")
     tiles = occ_ref.shape[0]
@@ -64,8 +64,13 @@
         return 0
 
     far = SIDE * (SIDE - 1)
+    lax.fori_loop(1, n_refl, greet_refl, 0)
+    arrive = [pltpu.make_async_copy(src, dst, in_sem.at[n]) for n, (src, dst) in enumerate(zip(sources, inputs))]
+    for copy in arrive:
+        copy.start()
     lax.fori_loop(0, far, greet_far, 0)
-    lax.fori_loop(1, n_refl, greet_refl, 0)
+    for copy in arrive:
+        copy.wait()
 
     rows[me_r] = miller_ref[...] + top
     ow[me_r, 0:1, :] = obs_ref[...]
@@ -175,6 +180,7 @@
     steps = 2 * n_refl
     per = 8
     chunks = steps // per
+    hand_on = steps - 6
 
     def to_column(src, q, slot):
         return pltpu.make_async_remote_copy(
@@ -217,23 +223,29 @@
         later = i - 2
         return jnp.where(i < 2, 2 * me_r + i, jnp.where(later < 2 * me_r, later, i))
 
+    def picks_copies():
+        return [pltpu.make_async_copy(idx_v.at[d, 0], picks[d], i_sem.at[d]) for d in range(3)]
+
     def prepare():
         all_of(rows, g_send, g_recv, n_refl - 1).wait_recv()
         for b in range(n_refl):
             for d in range(3):
                 idx_v[d, :, b * LANES : (b + 1) * LANES] = rows[b, d : d + 1, :]
-        copies = [pltpu.make_async_copy(idx_v.at[d, 0], picks[d], i_sem.at[d]) for d in range(3)]
-        for copy in copies:
+        for copy in picks_copies():
             copy.start()
         for b in range(n_refl):
             forms(b, pl.ds(b * LANES, LANES))
-        for copy in copies:
-            copy.wait()
 
     def forward_step(i, _):
         @pl.when(i == 2)
         def _():
             prepare()
+            for copy in picks_copies():
+                copy.wait()
+
+        @pl.when(i == hand_on)
+        def _():
+            send_plane(0)
 
         n = step_at(i)
         before = step_at(lax.rem(i + steps - 1, steps))
@@ -289,11 +301,10 @@
             seen[q, 2 * b : 2 * b + 1, :] = jnp.where(low_row, row, turned)
             seen[q, 2 * b + 1 : 2 * b + 2, :] = jnp.where(low_row, turned, row)
 
-    send_plane(0)
+    send_plane(1)
     for b in range(n_refl):
         for d, wide in enumerate((wide_h, wide_k, wide_l)):
             wide[b * LANES : (b + 1) * LANES, :] = spread((rows[b, d : d + 1, :] - top).astype(jnp.float32))
-    send_plane(1)
     send_plane(2)
 
     def totals(q):
@@ -348,15 +359,15 @@
     none = jnp.zeros((8, LANES), jnp.float32)
     group = ((none,) * (tiles // 8),) * 3
     size_q = per * half // unroll_b
-    known = [totals(0)]
-    both_sums(0, *known[0])
-    acc2 = lax.fori_loop(0, size_q // 4, early, (group, group))
-    send_plane(3)
-    acc2 = lax.fori_loop(size_q // 4, size_q, early, acc2)
-    known.append(totals(1))
-    both_sums(1, *known[1])
-    acc2 = lax.fori_loop(size_q, 2 * size_q, early, acc2)
-    known += [totals(q) for q in range(2, chunks)]
+    known = []
+    acc2 = (group, group)
+    for q in range(chunks - 1):
+        known.append(totals(q))
+        both_sums(q, *known[q])
+        acc2 = lax.fori_loop(q * size_q, (q + 1) * size_q, early, acc2)
+        if q == 0:
+            send_plane(chunks - 1)
+    known.append(totals(chunks - 1))
 
     over = sum(jnp.where(low, weight * obs * amp, 0.0) for _, amp, obs, weight in known)
     under = sum(jnp.where(low, weight * amp * amp, 0.0) for _, amp, obs, weight in known)
@@ -365,9 +376,9 @@
     scale = over / under
     for q, (both, amp, obs, weight) in enumerate(known):
         seen[0, q * per : (q + 1) * per, :] = scale * amp
-        if q >= 2:
+        if q == chunks - 1:
             place(q, factor * weight * scale * (scale * amp - obs) / amp * both, wide_a, wide_b)
-    acc = lax.fori_loop(2 * size_q, chunks * size_q, late, group)
+    acc = lax.fori_loop((chunks - 1) * size_q, chunks * size_q, late, group)
     for d in range(3):
         for v in range(tiles // 8):
             total = acc[d][v] + scale * (scale * acc2[0][d][v] - acc2[1][d][v])
@@ -391,7 +402,6 @@
         tiles = shard // LANES
         refl = miller.shape[1] * n_refl
         vmem = pl.BlockSpec(memory_space=pltpu.VMEM)
-        smem = pl.BlockSpec(memory_space=pltpu.SMEM)
         f32 = jnp.float32
         table = pltpu.VMEM((2 * top + 1, 2, tiles, LANES), f32)
         wide = pltpu.VMEM((refl, LANES), f32)
@@ -401,12 +411,22 @@
         gradient, residual = pl.pallas_call(
             functools.partial(kernel, n_atom, n_refl),
             out_shape=(
-                jax.ShapeDtypeStruct((3, shard), f32),
-                jax.ShapeDtypeStruct((1, LANES), f32),
+                pltpu.VMEM((3, shard), f32),
+                pltpu.VMEM((1, LANES), f32),
             ),
-            in_specs=[vmem] * 7 + [smem] * 3,
+            in_specs=[pl.BlockSpec(memory_space=pl.ANY)] * 10,
             out_specs=(vmem, vmem),
             scratch_shapes=[
+                pltpu.VMEM((3, shard), f32),
+                pltpu.VMEM((tiles, LANES), f32),
+                pltpu.VMEM((tiles, LANES), f32),
+                pltpu.VMEM((tiles, LANES), jnp.int32),
+                pltpu.VMEM((3, LANES), jnp.int32),
+                pltpu.VMEM((1, LANES), f32),
+                pltpu.VMEM((1, LANES), f32),
+                pltpu.SMEM((GAUSS, TYPES), f32),
+                pltpu.SMEM((GAUSS, TYPES), f32),
+                pltpu.SMEM((TYPES,), f32),
                 table, table, table,
                 pltpu.VMEM((refl, 2, tiles, LANES), f32),
                 wide,
@@ -422,7 +442,7 @@
                 wide, wide, wide, wide, wide, wide, wide,
                 dma, dma, dma, dma,
                 dma((chunks,)), dma((chunks,)), dma((chunks,)), dma((chunks,)),
-                dma((3,)), dma((3,)),
+                dma((3,)), dma((3,)), dma((10,)),
             ],
             compiler_params=pltpu.CompilerParams(
                 collective_id=0, has_side_effects=True, vmem_limit_bytes=58 * 2**20

time: 46.5 us -> 44.6 us (0.959)
  Pallas kernels: 43.7 us -> 42.6 us
  other arithmetic: 1.9 us -> 1.14 us
    pallas_call x1, Pallas kernels: 43.7 us -> 42.6 us  [local(): pl.pallas_call(functools.partial(kernel, n_atom, n_refl), out_shape=(pltp...]
    mul x1, other arithmetic: 1.38 us -> 0.62 us  [local(): return (gradient * (two_pi * inv_atoms), residual.reshape(LANES) - observed)]
where the time goes in v5:
time: 44.6 us; the launch traced here: 44.4 us
  Pallas kernels  42.6 us (96%)
  other arithmetic  1.14 us (3%)
  between operations  0.65 us (1%)
    pallas_call x1, Pallas kernels, local(): pl.pallas_call(functools.partial(kernel, n_atom, n_refl), out_shape=(pltp...  42.6 us

profile of v5, /device:TPU:1, one launch (start us, length us, event | category | flops | bytes accessed | tf_op | source)
XLA Modules:
  0.0 44.4 jit_solution(9247414894075272962)
XLA Ops:
  0.6 42.6 %shard_map.113 = (f32[3,2048]{1,0:T(4,128)S(1)}, f32[1,128]{1,0:T(1,128)S(1)}) custom-call(f32[3,2048]{1,0:T(4,128)} %refs_0_.1, f32[16,128]{1,0:T(8,128)} %bitcast.9, f32[16,128]{1,0:T(8,128)} %bitcast.10, s32[16,128]{1,0:T(8,128)} %bitcast.11, s32[3,128]{1,0:T(4,128)} %refs_4_.1, f32[1,128]{1,0:T(1,128)} %bitcast.15, f32[1,128]{1,0:T(1,128)} %bitcast.14, ...), custom_call_target="tpu_custom_call" | custom-call | tf_op jit(solution)/shard_map/pallas_call | solution.py:411
  43.3 0.0 copy-start
  43.3 0.6 %broadcast_multiply_fusion = f32[3,2048]{1,0:T(4,128)} fusion(f32[3,2048]{1,0:T(4,128)S(1)} %get-tuple-element.4), kind=kLoop, calls=%fused_computation | loop fusion | flops 6144 | bytes 49152 | tf_op jit(solution)/shard_map/mul | solution.py:461
  43.9 0.0 copy-done
  43.9 0.5 %bitcast_subtract_fusion = f32[128]{0:T(128)} fusion(f32[128]{0:T(128)S(1)} %copy-done, f32[1,128]{1,0:T(1,128)S(1)} %get-tuple-element.5), kind=kLoop, calls=%fused_computation.1 | loop fusion | flops 128 | bytes 1536 | tf_op jit(solution)/shard_map/sub | solution.py:461
Async XLA Ops:
  43.3 0.7 %copy-start = (f32[128]{0:T(128)S(1)}, f32[128]{0:T(128)}, u32[]{:S(2)}) copy-start(f32[128]{0:T(128)} %param.15) | copy-start | bytes 1540

commit v6 on v5

--- a/solution.py
+++ b/solution.py
@@ -42,33 +42,28 @@
     column = z * SIDE + zc
     plane = x * SIDE + y
 
-    def column_peer(slot):
-        return x * SIDE + lax.rem(slot, SIDE), lax.div(slot, SIDE) * SIDE + y
-
-    def plane_peer(slot):
-        return lax.div(slot, SIDE) * SIDE + zc, z * SIDE + lax.rem(slot, SIDE)
+    xs, zcs, zs, ys = ([lax.rem(at + turn, SIDE) for turn in range(SIDE)] for at in (x, zc, z, y))
+    turns = [(i, j) for i in range(SIDE) for j in range(SIDE) if i or j]
+    refl_peers = [(me_a, zs[i] * SIDE + ys[j]) for i, j in turns]
+    column_peers = [(x * SIDE + zcs[j], zs[i] * SIDE + y) for i, j in turns]
+    plane_peers = [(xs[i] * SIDE + zc, z * SIDE + ys[j]) for i, j in turns]
 
     barrier = pltpu.get_barrier_semaphore()
 
     def greet(peer):
         pl.semaphore_signal(barrier, inc=1, device_id=peer, device_id_type=MESH)
 
-    def greet_far(i, _):
-        turn, other = 1 + lax.div(i, SIDE), lax.rem(i, SIDE)
-        greet(column_peer(other * SIDE + lax.rem(zc + turn, SIDE)))
-        greet(plane_peer(lax.rem(x + turn, SIDE) * SIDE + other))
-        return 0
-
-    def greet_refl(s, _):
-        greet((me_a, lax.rem(me_r + s, n_refl)))
-        return 0
-
     far = SIDE * (SIDE - 1)
-    lax.fori_loop(1, n_refl, greet_refl, 0)
+    for peer in refl_peers:
+        greet(peer)
     arrive = [pltpu.make_async_copy(src, dst, in_sem.at[n]) for n, (src, dst) in enumerate(zip(sources, inputs))]
     for copy in arrive:
         copy.start()
-    lax.fori_loop(0, far, greet_far, 0)
+    for (i, j), over_column, over_plane in zip(turns, column_peers, plane_peers):
+        if j:
+            greet(over_column)
+        if i:
+            greet(over_plane)
     for copy in arrive:
         copy.wait()
 
@@ -82,26 +77,18 @@
 
     pl.semaphore_wait(barrier, n_refl - 1 + 2 * far)
 
-    def to_refl(src, dst, send, recv, peer):
+    def to_refl(src, send, recv, peer):
         return pltpu.make_async_remote_copy(
-            src_ref=src, dst_ref=dst, send_sem=send, recv_sem=recv,
-            device_id=(me_a, peer), device_id_type=MESH,
+            src_ref=src, dst_ref=src, send_sem=send, recv_sem=recv, device_id=peer, device_id_type=MESH
         )
 
     def all_of(ref, send, recv, count):
-        part_of = ref.at[pl.ds(0, count)]
-        return to_refl(part_of, part_of, send, recv, me_r)
-
-    def g_start(s, _):
-        to_refl(rows.at[me_r], rows.at[me_r], g_send, g_recv, lax.rem(me_r + s, n_refl)).start()
-        return 0
-
-    def o_start(s, _):
-        to_refl(ow.at[me_r], ow.at[me_r], o_send, o_recv, lax.rem(me_r + s, n_refl)).start()
-        return 0
-
-    lax.fori_loop(1, n_refl, g_start, 0)
-    lax.fori_loop(1, n_refl, o_start, 0)
+        return to_refl(ref.at[pl.ds(0, count)], send, recv, refl_peers[0])
+
+    for peer in refl_peers:
+        to_refl(rows.at[me_r], g_send, g_recv, peer).start()
+    for peer in refl_peers:
+        to_refl(ow.at[me_r], o_send, o_recv, peer).start()
 
     first = []
     for d in range(3):
@@ -182,42 +169,33 @@
     chunks = steps // per
     hand_on = steps - 6
 
-    def to_column(src, q, slot):
+    def to_column(src, q, peer):
         return pltpu.make_async_remote_copy(
             src_ref=src, dst_ref=src, send_sem=c_send.at[q], recv_sem=c_recv.at[q],
-            device_id=column_peer(slot), device_id_type=MESH,
+            device_id=peer, device_id_type=MESH,
         )
 
-    def to_plane(src, q, slot):
+    def to_plane(src, q, peer):
         return pltpu.make_async_remote_copy(
             src_ref=src, dst_ref=src, send_sem=p_send.at[q], recv_sem=p_recv.at[q],
-            device_id=plane_peer(slot), device_id_type=MESH,
+            device_id=peer, device_id_type=MESH,
         )
 
-    peers = SIDE * SIDE
-
     def rest_column(q):
-        return to_column(in_column.at[q, pl.ds(0, peers - 1)], q, column)
+        return to_column(in_column.at[q, pl.ds(0, len(turns))], q, column_peers[0])
 
     def rest_plane(q):
-        return to_plane(in_plane.at[q, pl.ds(0, peers - 1)], q, plane)
+        return to_plane(in_plane.at[q, pl.ds(0, len(turns))], q, plane_peers[0])
 
     def send_column(q):
-        def one(s, _):
-            to_column(in_column.at[q, column], q, lax.rem(column + s, peers)).start()
-            return 0
-
-        lax.fori_loop(1, peers, one, 0)
+        for peer in column_peers:
+            to_column(in_column.at[q, column], q, peer).start()
 
     def send_plane(q):
         rest_column(q).wait_recv()
         in_plane[q, plane] = jnp.sum(in_column[q], axis=0)
-
-        def one(s, _):
-            to_plane(in_plane.at[q, plane], q, lax.rem(plane + s, peers)).start()
-            return 0
-
-        lax.fori_loop(1, peers, one, 0)
+        for peer in plane_peers:
+            to_plane(in_plane.at[q, plane], q, peer).start()
 
     def step_at(i):
         later = i - 2

time: 44.6 us -> 43.2 us (0.969)
  Pallas kernels: 42.6 us -> 41.2 us
    pallas_call x1, Pallas kernels: 42.6 us -> 41.2 us  [local(): pl.pallas_call(functools.partial(kernel, n_atom, n_refl), out_shape=(pltp...]
where the time goes in v6:
time: 43.2 us; the launch traced here: 43 us
  Pallas kernels  41.2 us (95%)
  other arithmetic  1.14 us (3%)
  between operations  0.65 us (2%)
    pallas_call x1, Pallas kernels, local(): pl.pallas_call(functools.partial(kernel, n_atom, n_refl), out_shape=(pltp...  41.2 us

profile of v6, /device:TPU:1, one launch (start us, length us, event | category | flops | bytes accessed | tf_op | source)
XLA Modules:
  0.0 43.0 jit_solution(9067019113095032969)
XLA Ops:
  0.6 41.2 %shard_map.113 = (f32[3,2048]{1,0:T(4,128)S(1)}, f32[1,128]{1,0:T(1,128)S(1)}) custom-call(f32[3,2048]{1,0:T(4,128)} %refs_0_.1, f32[16,128]{1,0:T(8,128)} %bitcast.9, f32[16,128]{1,0:T(8,128)} %bitcast.10, s32[16,128]{1,0:T(8,128)} %bitcast.11, s32[3,128]{1,0:T(4,128)} %refs_4_.1, f32[1,128]{1,0:T(1,128)} %bitcast.15, f32[1,128]{1,0:T(1,128)} %bitcast.14, ...), custom_call_target="tpu_custom_call" | custom-call | tf_op jit(solution)/shard_map/pallas_call | solution.py:389
  41.8 0.0 copy-start
  41.8 0.6 %broadcast_multiply_fusion = f32[3,2048]{1,0:T(4,128)} fusion(f32[3,2048]{1,0:T(4,128)S(1)} %get-tuple-element.4), kind=kLoop, calls=%fused_computation | loop fusion | flops 6144 | bytes 49152 | tf_op jit(solution)/shard_map/mul | solution.py:439
  42.5 0.0 copy-done
  42.5 0.5 %bitcast_subtract_fusion = f32[128]{0:T(128)} fusion(f32[128]{0:T(128)S(1)} %copy-done, f32[1,128]{1,0:T(1,128)S(1)} %get-tuple-element.5), kind=kLoop, calls=%fused_computation.1 | loop fusion | flops 128 | bytes 1536 | tf_op jit(solution)/shard_map/sub | solution.py:439
Async XLA Ops:
  41.8 0.7 %copy-start = (f32[128]{0:T(128)S(1)}, f32[128]{0:T(128)}, u32[]{:S(2)}) copy-start(f32[128]{0:T(128)} %param.15) | copy-start | bytes 1540

commit v7 on v6

--- a/solution.py
+++ b/solution.py
@@ -87,9 +87,6 @@
 
     for peer in refl_peers:
         to_refl(rows.at[me_r], g_send, g_recv, peer).start()
-    for peer in refl_peers:
-        to_refl(ow.at[me_r], o_send, o_recv, peer).start()
-
     first = []
     for d in range(3):
         coord = jnp.concatenate([pos_ref[d : d + 1, a * LANES : (a + 1) * LANES] for a in range(tiles)], axis=0)
@@ -115,6 +112,9 @@
     one = jnp.ones((tiles, LANES), jnp.float32)
     zero = jnp.zeros((tiles, LANES), jnp.float32)
     lax.fori_loop(0, top + 1, table_step, (one, zero) * 3)
+
+    for peer in refl_peers:
+        to_refl(ow.at[me_r], o_send, o_recv, peer).start()
 
     kind_row = lax.broadcasted_iota(jnp.int32, (TYPES, LANES), 0)
 
@@ -342,9 +342,11 @@
     for q in range(chunks - 1):
         known.append(totals(q))
         both_sums(q, *known[q])
-        acc2 = lax.fori_loop(q * size_q, (q + 1) * size_q, early, acc2)
-        if q == 0:
+        middle = q * size_q + size_q // 2
+        acc2 = lax.fori_loop(q * size_q, middle, early, acc2)
+        if q == 1:
             send_plane(chunks - 1)
+        acc2 = lax.fori_loop(middle, (q + 1) * size_q, early, acc2)
     known.append(totals(chunks - 1))
 
     over = sum(jnp.where(low, weight * obs * amp, 0.0) for _, amp, obs, weight in known)

time: 43.2 us -> 43.3 us (level)
  no operation moved by 1% of the time
where the time goes in v7:
time: 43.3 us; the launch traced here: 43.1 us
  Pallas kernels  41.3 us (95%)
  other arithmetic  1.14 us (3%)
  between operations  0.65 us (2%)
    pallas_call x1, Pallas kernels, local(): pl.pallas_call(functools.partial(kernel, n_atom, n_refl), out_shape=(pltp...  41.3 us

profile of v7, /device:TPU:1, one launch (start us, length us, event | category | flops | bytes accessed | tf_op | source)
XLA Modules:
  0.0 43.1 jit_solution(6468619920008818758)
XLA Ops:
  0.6 41.3 %shard_map.113 = (f32[3,2048]{1,0:T(4,128)S(1)}, f32[1,128]{1,0:T(1,128)S(1)}) custom-call(f32[3,2048]{1,0:T(4,128)} %refs_0_.1, f32[16,128]{1,0:T(8,128)} %bitcast.9, f32[16,128]{1,0:T(8,128)} %bitcast.10, s32[16,128]{1,0:T(8,128)} %bitcast.11, s32[3,128]{1,0:T(4,128)} %refs_4_.1, f32[1,128]{1,0:T(1,128)} %bitcast.15, f32[1,128]{1,0:T(1,128)} %bitcast.14, ...), custom_call_target="tpu_custom_call" | custom-call | tf_op jit(solution)/shard_map/pallas_call | solution.py:391
  42.0 0.0 copy-start
  42.0 0.6 %broadcast_multiply_fusion = f32[3,2048]{1,0:T(4,128)} fusion(f32[3,2048]{1,0:T(4,128)S(1)} %get-tuple-element.4), kind=kLoop, calls=%fused_computation | loop fusion | flops 6144 | bytes 49152 | tf_op jit(solution)/shard_map/mul | solution.py:441
  42.6 0.0 copy-done
  42.6 0.5 %bitcast_subtract_fusion = f32[128]{0:T(128)} fusion(f32[128]{0:T(128)S(1)} %copy-done, f32[1,128]{1,0:T(1,128)S(1)} %get-tuple-element.5), kind=kLoop, calls=%fused_computation.1 | loop fusion | flops 128 | bytes 1536 | tf_op jit(solution)/shard_map/sub | solution.py:441
Async XLA Ops:
  42.0 0.7 %copy-start = (f32[128]{0:T(128)S(1)}, f32[128]{0:T(128)}, u32[]{:S(2)}) copy-start(f32[128]{0:T(128)} %param.15) | copy-start | bytes 1540
